TPU v7x, 32 devices: a whole 2x2x4 slice. The times are simulated.
32 devices in a mesh: fsdp: 4 (over y, x), ctx: 2 (over core), tp: 4 (over z).
Axes of the slice: x: 2, y: 2, z: 4, core: 2. Of those that a mesh axis runs over, the one named last changes fastest.
Arguments:
- tokens: bfloat16 [12, 640, 1024], P('fsdp', 'ctx')
- lengths: int32 [12, 2], P('fsdp'), may hold values from 257 to 320, as said below
- image_count: int32 [4], P('fsdp'), may hold values from 1 to 3, as said below
- qkv_weight: bfloat16 [2, 1024, 3, 1024], P(None, 'fsdp', None, 'tp')
- qv_bias: bfloat16 [2, 2, 4, 256], P(None, None, 'tp', 'fsdp'), may hold values from -0.59765625 to 0.59765625
- out_weight: bfloat16 [2, 1024, 1024], P(None, 'tp', 'fsdp')
- out_bias: bfloat16 [2, 1024], P(None, 'fsdp'), may hold values from -1.796875 to 1.796875
- up_weight: bfloat16 [2, 1024, 4096], P(None, 'fsdp', 'tp')
- up_bias: bfloat16 [2, 4, 1024], P(None, 'tp', 'fsdp'), may hold values from -1.796875 to 1.796875
- down_weight: bfloat16 [2, 4096, 1024], P(None, 'tp', 'fsdp')
- down_bias: bfloat16 [2, 1024], P(None, 'fsdp'), may hold values from -1.796875 to 1.796875
- gain_one: bfloat16 [2, 1024], P(None, 'fsdp'), may hold values from 0.5 to 1.5
- gain_two: bfloat16 [2, 1024], P(None, 'fsdp'), may hold values from 0.5 to 1.5
- cotangent: bfloat16 [12, 640, 1024], P('fsdp', 'ctx')
Outputs:
- output: bfloat16 [12, 640, 1024], P('fsdp', 'ctx')
- input_grad: bfloat16 [12, 640, 1024], P('fsdp', 'ctx')
- qkv_weight_grad: float32 [2, 1024, 3, 1024], P(None, 'fsdp', None, 'tp')
- qv_bias_grad: float32 [2, 2, 4, 256], P(None, None, 'tp', 'fsdp')
- out_weight_grad: float32 [2, 1024, 1024], P(None, 'tp', 'fsdp')
- out_bias_grad: float32 [2, 1024], P(None, 'fsdp')
- up_weight_grad: float32 [2, 1024, 4096], P(None, 'fsdp', 'tp')
- up_bias_grad: float32 [2, 4, 1024], P(None, 'tp', 'fsdp')
- down_weight_grad: float32 [2, 4096, 1024], P(None, 'tp', 'fsdp')
- down_bias_grad: float32 [2, 1024], P(None, 'fsdp')
- gain_one_grad: float32 [2, 1024], P(None, 'fsdp')
- gain_two_grad: float32 [2, 1024], P(None, 'fsdp')
Inputs may be any that keep to these rules, and one draw needn't show every extreme that they name: `lengths`: in each image one index of ctx, drawn from the seed, holds exactly 320 tokens; the other indices share the remaining 577 - 320 tokens as evenly as possible; each image's counts sum to 577. Slots 0 to image_count - 1 of an fsdp index hold images; some index holds 3.
All inputs are finite; a program needn't handle non-finite values.
Results may differ from a plain program's by a relative error of at most 0.02.
Values may be sent and summed in bfloat16 or wider, within the bound.
No kernel may reach another device: no remote copies, remote signals or barrier semaphores. Data moves between devices by JAX's collectives and lax.ppermute only.
A program may use at most 192 MiB of HBM per device.

v0:
```python
import jax
import jax.numpy as jnp
from jax import lax
from jax.sharding import PartitionSpec as P

HD = 64
SEQ = 577
BF = jnp.bfloat16
F32 = jnp.float32


def layer_norm(vectors, scaling):
    centre = vectors - jnp.mean(vectors, axis=-1, keepdims=True)
    spread = jnp.mean(centre * centre, axis=-1, keepdims=True)
    return centre * lax.rsqrt(spread + 1e-06) * scaling


def gelu_exact(values):
    return 0.5 * values * (1.0 + lax.erf(values * 0.7071067811865476))


X_PAIRS = [(0, 1), (1, 0), (2, 3), (3, 2)]
Y_PAIRS = [(0, 2), (2, 0), (1, 3), (3, 1)]


def square():
    return lax.axis_size("fsdp") == 4


def reorder(values):
    if not square():
        return values
    place = lax.axis_index("fsdp")
    lead = values.shape[:-1]
    blocks = values.reshape(lead + (2, 2, values.shape[-1] // 4))
    blocks = jnp.where(place % 2 == 1, blocks[..., :, ::-1, :], blocks)
    blocks = jnp.where(place >= 2, blocks[..., ::-1, :, :], blocks)
    return blocks.reshape(values.shape)


def send_x(values):
    return lax.ppermute(values, "fsdp", X_PAIRS)


def send_y(values):
    return lax.ppermute(values, "fsdp", Y_PAIRS)


def swap(values):
    return lax.ppermute(values, "ctx", [(0, 1), (1, 0)])


def both_cores(partial_sum):
    low = partial_sum.astype(BF)
    return low.astype(F32) + swap(low).astype(F32)


def gather_rows(shard):
    if not square():
        return lax.all_gather(shard, "fsdp", axis=0, tiled=True)
    half = shard.shape[0] // 2
    from_x, from_y = (send_x(shard), send_y(shard))
    far_a, far_b = (send_y(from_x[:half]), send_x(from_y[half:]))
    return jnp.concatenate([shard, from_x, from_y, far_a, far_b], axis=0)


def scatter_rows(full):
    if not square():
        return lax.psum_scatter(full.astype(BF), "fsdp", scatter_dimension=0, tiled=True).astype(
            F32
        )
    rows = full.shape[0] // 4
    half = rows // 2
    own, to_x, to_y, far = [full[k * rows : (k + 1) * rows] for k in range(4)]
    first = send_x(jnp.concatenate([to_x[:half], far[:half]]).astype(BF)).astype(F32)
    second = send_y(jnp.concatenate([to_y[half:], far[half:]]).astype(BF)).astype(F32)
    own_a = own[:half] + first[:half]
    own_b = own[half:] + second[:half]
    pass_y = (to_y[:half] + first[half:]).astype(BF)
    pass_x = (to_x[half:] + second[half:]).astype(BF)
    own_a = own_a + send_y(pass_y).astype(F32)
    own_b = own_b + send_x(pass_x).astype(F32)
    return jnp.concatenate([own_a, own_b])


def gather_matrix(shard, place):
    rows, groups, columns = shard.shape
    half = lax.dynamic_index_in_dim(
        shard.reshape(rows, groups, 2, columns // 2), place, 2, keepdims=False
    )
    along = lax.all_gather(half, "tp", axis=0)
    along = jnp.transpose(along, (1, 2, 0, 3)).reshape(rows, -1)
    return gather_rows(along)


def scatter_matrix(grad, groups, place):
    count = lax.axis_size("tp")
    kept = scatter_rows(grad).astype(BF)
    rows = kept.shape[0]
    kept = jnp.transpose(kept.reshape(rows, groups, count, -1), (2, 0, 1, 3))
    own = lax.psum_scatter(kept, "tp", scatter_dimension=0, tiled=False)
    other = swap(own)
    low = jnp.where(place == 0, own, other)
    high = jnp.where(place == 0, other, own)
    return jnp.concatenate([low, high], axis=-1).astype(F32)


def heads_of(values):
    return values.reshape(values.shape[0], -1, HD)


def masked_scores(queries, keys, key_valid):
    scores = jnp.einsum("qhd,khd->hqk", queries, keys, preferred_element_type=F32) * HD ** (-0.5)
    return jnp.where(key_valid, scores, -1000000000.0)


def mm(left, right):
    return jnp.dot(left, right, preferred_element_type=F32)


def mm_nt(left, right):
    return lax.dot_general(left, right, (((1,), (1,)), ((), ())), preferred_element_type=F32)


def mm_tn(left, right):
    return lax.dot_general(left, right, (((0,), (0,)), ((), ())), preferred_element_type=F32)


def forward_layer(stream, weights, vectors, key_valid):
    qkv, out, up, down = weights
    shift_q, shift_v, out_shift, up_shift, down_shift, gain_first, gain_second = vectors
    normed = layer_norm(stream, gain_first).astype(BF)
    project = mm(normed, qkv)
    width = project.shape[1] // 3
    queries = heads_of((project[:, :width] + shift_q).astype(BF))
    keys = heads_of(project[:, width : 2 * width].astype(BF))
    values = heads_of((project[:, 2 * width :] + shift_v).astype(BF))
    scores = masked_scores(queries, keys, key_valid)
    highest = jnp.max(scores, axis=-1, keepdims=True)
    exponent = jnp.exp(scores - highest)
    denominator = jnp.sum(exponent, axis=-1, keepdims=True)
    probs = (exponent / denominator).astype(BF)
    log_total = highest + jnp.log(denominator)
    mixed = jnp.einsum("hqk,khd->qhd", probs, values, preferred_element_type=F32).astype(BF)
    mixed = mixed.reshape(stream.shape[0], width)
    middle = stream + both_cores(mm_nt(mixed, out)) + out_shift
    normed_b = layer_norm(middle, gain_second).astype(BF)
    hidden = mm(normed_b, up) + up_shift
    active = gelu_exact(hidden).astype(BF)
    following = middle + both_cores(mm_nt(active, down)) + down_shift
    return (
        following,
        (stream, normed, queries, keys, values, log_total, mixed, middle, normed_b, hidden, active),
    )


def backward_layer(gradient, saved, weights, vectors, key_valid, emit):
    qkv, out, up, down = weights
    gain_first, gain_second = vectors[5:]
    stream, normed, queries, keys, values, log_total, mixed, middle, normed_b, hidden, active = (
        saved
    )
    total = lambda array: jnp.sum(array.astype(F32), axis=0)
    grad_low = gradient.astype(BF)
    emit("down", mm_tn(grad_low, active))
    delta_hidden = jax.vjp(gelu_exact, hidden)[1](mm(grad_low, down))[0].astype(BF)
    emit("up", mm_tn(normed_b, delta_hidden))
    delta_normed_b = both_cores(mm_nt(delta_hidden, up))
    back_middle, delta_gain_second = jax.vjp(layer_norm, middle, gain_second)[1](delta_normed_b)
    grad_middle = gradient + back_middle
    grad_attend = grad_middle.astype(BF)
    emit("out", mm_tn(grad_attend, mixed))
    delta_mixed = heads_of(mm(grad_attend, out).astype(BF))
    probs = jnp.exp(masked_scores(queries, keys, key_valid) - log_total)
    delta_values = jnp.einsum(
        "hqk,qhd->khd", probs.astype(BF), delta_mixed, preferred_element_type=F32
    ).astype(BF)
    delta_probs = jnp.einsum("qhd,khd->hqk", delta_mixed, values, preferred_element_type=F32)
    inner = jnp.sum(probs * delta_probs, axis=-1, keepdims=True)
    delta_scores = (probs * (delta_probs - inner)).astype(BF)
    scale = HD ** (-0.5)
    delta_queries = (
        jnp.einsum("hqk,khd->qhd", delta_scores, keys, preferred_element_type=F32) * scale
    ).astype(BF)
    delta_keys = (
        jnp.einsum("hqk,qhd->khd", delta_scores, queries, preferred_element_type=F32) * scale
    ).astype(BF)
    flat = [
        piece.reshape(stream.shape[0], -1) for piece in (delta_queries, delta_keys, delta_values)
    ]
    delta_project = jnp.concatenate(flat, axis=1)
    emit("qkv", mm_tn(normed, delta_project))
    delta_normed = both_cores(mm_nt(delta_project, qkv))
    back_stream, delta_gain_first = jax.vjp(layer_norm, stream, gain_first)[1](delta_normed)
    sums = (
        total(flat[0]),
        total(flat[2]),
        total(grad_attend),
        total(delta_hidden),
        total(grad_low),
        delta_gain_first,
        delta_gain_second,
    )
    return (grad_middle + back_stream, sums)


def shards(
    tokens,
    lengths,
    image_count,
    qkv_weight,
    qv_bias,
    out_weight,
    out_bias,
    up_weight,
    up_bias,
    down_weight,
    down_bias,
    gain_one,
    gain_two,
    cotangent,
):
    slots, capacity, features = tokens.shape
    layers = qkv_weight.shape[0]
    n_fsdp, n_tp = (lax.axis_size("fsdp"), lax.axis_size("tp"))
    assert lax.axis_size("ctx") == 2 and slots <= n_tp
    group, core, lane = (lax.axis_index("fsdp"), lax.axis_index("ctx"), lax.axis_index("tp"))
    rows = -(-SEQ // 16) * 16
    slot = jnp.minimum(lane, slots - 1)
    own_lengths = lax.dynamic_index_in_dim(lengths, slot, 0, keepdims=False)
    live = lane < jnp.minimum(image_count[0], slots)
    key_valid = (jnp.arange(rows) < SEQ)[None, None, :]
    row_mask = ((jnp.arange(rows) < SEQ) & live).astype(F32)[:, None]
    pieces = (qv_bias, up_bias, out_bias, down_bias, gain_one, gain_two)
    packed = jnp.concatenate([piece.reshape(-1) for piece in pieces])
    spread = lax.all_gather(packed, ("fsdp", "tp"), axis=0).reshape(n_fsdp, n_tp, -1)
    found, start = ([], 0)
    for piece in pieces:
        found.append(spread[:, :, start : start + piece.size])
        start += piece.size

    def by_core(array, count):
        array = array.reshape(n_fsdp, n_tp, layers, count, -1)
        array = jnp.transpose(array, (2, 3, 1, 0, 4)).reshape(layers, count, n_tp, 2, -1)
        return lax.dynamic_index_in_dim(array, core, 3, keepdims=False).reshape(layers, count, -1)

    def by_feature(array):
        array = array[:, 0].reshape(n_fsdp, layers, -1)
        return reorder(jnp.transpose(array, (1, 0, 2)).reshape(layers, features))

    qv_all, up_all = (by_core(found[0], 2), by_core(found[1], 1))
    out_all, down_all, one_all, two_all = [by_feature(array) for array in found[2:]]
    vectors = [
        (qv_all[l, 0], qv_all[l, 1], out_all[l], up_all[l, 0], down_all[l], one_all[l], two_all[l])
        for l in range(layers)
    ]
    weights = []
    for l in range(layers):
        raw = (
            qkv_weight[l],
            out_weight[l].T[:, None],
            up_weight[l][:, None],
            down_weight[l].T[:, None],
        )
        weights.append(tuple((gather_matrix(piece, core) for piece in raw)))
    own_pair = jnp.stack(
        [lax.dynamic_index_in_dim(a, slot, 0, keepdims=False) for a in (tokens, cotangent)]
    )
    other_pair = swap(own_pair)
    low = jnp.where(core == 0, own_pair, other_pair)
    high = jnp.where(core == 0, other_pair, own_pair)
    image = jnp.concatenate([low, jnp.zeros_like(low)], axis=1)
    image = lax.dynamic_update_slice_in_dim(image, high, own_lengths[0], 1)[:, :rows]
    image = reorder(image).astype(F32)
    stream = image[0]
    saved = []
    for l in range(layers):
        stream, items = forward_layer(stream, weights[l], vectors[l], key_valid)
        saved.append(items)
    own_length = own_lengths[core]
    own_rows = ((jnp.arange(capacity) < own_length) & live)[:, None]

    def give_back(values):
        values = jnp.pad(reorder(values.astype(BF)), ((0, 2 * capacity - rows), (0, 0)))
        mine = lax.dynamic_slice_in_dim(
            values, jnp.where(core == 0, 0, own_lengths[0]), capacity, 0
        )
        mine = jnp.where(own_rows, mine, jnp.zeros_like(mine))
        return lax.all_gather(mine, "tp", axis=0)[:slots]

    output = give_back(stream)
    gradient = image[1] * row_mask
    grads = {}
    sums = [None] * layers
    for l in reversed(range(layers)):

        def emit(name, grad, l=l):
            grads[name, l] = scatter_matrix(grad, 3 if name == "qkv" else 1, core)

        gradient, sums[l] = backward_layer(
            gradient, saved[l], weights[l], vectors[l], key_valid, emit
        )
    input_grad = give_back(gradient)

    def from_core(array, count):
        array = array.reshape(layers, count, n_tp, 1, -1)
        mask = (jnp.arange(2) == core)[:, None]
        return jnp.where(mask, array, 0.0).reshape(layers * count, -1)

    first = (core == 0).astype(F32)
    member = lambda k: jnp.stack([sums[l][k] for l in range(layers)])
    joined = [
        from_core(jnp.stack([member(0), member(1)], axis=1), 2),
        from_core(member(3)[:, None], 1),
    ] + [reorder(member(k)) * first for k in (2, 4, 5, 6)]
    summed = lax.psum(jnp.concatenate([a.reshape(-1) for a in joined]), ("fsdp", "ctx", "tp"))
    whole, start = ([], 0)
    for a in joined:
        whole.append(summed[start : start + a.size])
        start += a.size
    pick = lambda a, i, axis: lax.dynamic_index_in_dim(a, i, axis, keepdims=True)
    qv_grad = pick(pick(whole[0].reshape(layers, 2, n_tp, n_fsdp, -1), lane, 2), group, 3)[
        :, :, :, 0
    ]
    up_grad = pick(pick(whole[1].reshape(layers, n_tp, n_fsdp, -1), lane, 1), group, 2)[:, :, 0]
    out_shift, down_shift, one, two = [
        pick(a.reshape(layers, n_fsdp, -1), group, 1)[:, 0] for a in whole[2:]
    ]
    stacked = lambda name: jnp.stack([grads[name, l] for l in range(layers)])
    qkv_grad = stacked("qkv")
    out_grad = jnp.swapaxes(stacked("out")[:, :, 0], 1, 2)
    up_w_grad = stacked("up")[:, :, 0]
    down_grad = jnp.swapaxes(stacked("down")[:, :, 0], 1, 2)
    return (
        output,
        input_grad,
        qkv_grad,
        qv_grad,
        out_grad,
        out_shift,
        up_w_grad,
        up_grad,
        down_grad,
        down_shift,
        one,
        two,
    )


def solution(mesh):
    in_specs = (
        P("fsdp", "ctx", None),
        P("fsdp", None),
        P("fsdp"),
        P(None, "fsdp", None, "tp"),
        P(None, None, "tp", "fsdp"),
        P(None, "tp", "fsdp"),
        P(None, "fsdp"),
        P(None, "fsdp", "tp"),
        P(None, "tp", "fsdp"),
        P(None, "tp", "fsdp"),
        P(None, "fsdp"),
        P(None, "fsdp"),
        P(None, "fsdp"),
        P("fsdp", "ctx", None),
    )
    out_specs = (
        P("fsdp", "ctx", None),
        P("fsdp", "ctx", None),
        P(None, "fsdp", None, "tp"),
        P(None, None, "tp", "fsdp"),
        P(None, "tp", "fsdp"),
        P(None, "fsdp"),
        P(None, "fsdp", "tp"),
        P(None, "tp", "fsdp"),
        P(None, "tp", "fsdp"),
        P(None, "fsdp"),
        P(None, "fsdp"),
        P(None, "fsdp"),
    )
    return jax.shard_map(shards, mesh=mesh, in_specs=in_specs, out_specs=out_specs, check_vma=False)
```

profile of v0, /device:TPU:0, one launch (start us, length us, event | category | flops | bytes accessed | tf_op | source)
XLA Modules:
  0.0 1221.1 jit_solution(7200938606107575798)
XLA Ops:
  11.6 16.6 %all-gather.6 = bf16[1024,1,1,128]{0,3,2,1:T(8,128)(2,1)S(1)} all-gather(bf16[256,1,1,128]{0,3,2,1:T(8,128)(2,1)S(1)} %constant_dynamic-slice_fusion.8), channel_id=8, replica_groups=mesh['fsdp'=4,'ctx'=2,'tp'=4] {'tp'}, dimensions={0}, use_global_device_ids=true | all-gather | bytes 327680 | tf_op jit(solution)/shard_map/all_gather | solution.py:91
  31.9 16.8 %all-gather.2 = bf16[1024,1,1,128]{0,3,2,1:T(8,128)(2,1)S(1)} all-gather(bf16[256,1,1,128]{0,3,2,1:T(8,128)(2,1)S(1)} %constant_dynamic-slice_fusion.12), channel_id=4, replica_groups=mesh['fsdp'=4,'ctx'=2,'tp'=4] {'tp'}, dimensions={0}, use_global_device_ids=true | all-gather | bytes 327680 | tf_op jit(solution)/shard_map/all_gather | solution.py:91
  50.7 24.3 %all-gather.5 = bf16[1024,3,1,128]{0,3,2,1:T(8,128)(2,1)S(1)} all-gather(bf16[256,3,1,128]{0,3,2,1:T(8,128)(2,1)S(1)} %constant_dynamic-slice_fusion.9), channel_id=7, replica_groups=mesh['fsdp'=4,'ctx'=2,'tp'=4] {'tp'}, dimensions={0}, use_global_device_ids=true | all-gather | bytes 983040 | tf_op jit(solution)/shard_map/all_gather | solution.py:91
  80.7 39.9 %all-gather.11 = bf16[16,1,2816]{2,1,0:T(2,128)(2,1)S(1)} all-gather(bf16[1,1,2816]{2,1,0:T(2,128)(2,1)S(1)} %reshape.1168), channel_id=2, replica_groups=mesh['fsdp'=4,'ctx'=2,'tp'=4] {'fsdp','tp'}, dimensions={0}, use_global_device_ids=true | all-gather | bytes 95744 | tf_op jit(solution)/shard_map/all_gather | solution.py:236
  126.1 19.7 %all-gather.1 = bf16[1024,3,1,128]{0,3,2,1:T(8,128)(2,1)S(1)} all-gather(bf16[256,3,1,128]{0,3,2,1:T(8,128)(2,1)S(1)} %constant_dynamic-slice_fusion.13), channel_id=3, replica_groups=mesh['fsdp'=4,'ctx'=2,'tp'=4] {'tp'}, dimensions={0}, use_global_device_ids=true | all-gather | bytes 983040 | tf_op jit(solution)/shard_map/all_gather | solution.py:91
  173.7 6.3 collective-permute-done.25
  206.0 6.9 collective-permute-done.3
  216.1 9.5 dynamic_update_slice.3
  227.3 5.7 reshape.1095
  233.0 19.4 %rev.66 = bf16[2,592,2,2,256]{4,3,2,1,0:T(2,128)(2,1)} reverse(bf16[2,592,2,2,256]{4,3,2,1,0:T(2,128)(2,1)S(1)} %reshape.1095), dimensions={3} | reverse | bytes 4849664 | tf_op jit(solution)/shard_map/rev | solution.py:36
  257.4 5.0 fusion.120
  262.4 3.5 squeeze.95
  266.4 4.5 fusion.106
  277.8 3.6 fusion.134
  291.0 4.3 squeeze.100
  303.9 3.4 collective-permute-start.14
  326.4 27.2 %collective-permute-done.10 = bf16[256,2048]{0,1:T(8,128)(2,1)} collective-permute-done((bf16[256,2048]{0,1:T(8,128)(2,1)}, bf16[256,2048]{0,1:T(8,128)(2,1)}, u32[]{:S(2)}, u32[]{:S(2)}) %collective-permute-start.10) | collective-permute-done | bytes 1048608 | tf_op jit(solution)/shard_map/ppermute | solution.py:42
  367.7 16.9 %collective-permute-done.12 = bf16[128,2048]{0,1:T(8,128)(2,1)S(1)} collective-permute-done((bf16[128,2048]{0,1:T(8,128)(2,1)S(1)}, bf16[128,2048]{0,1:T(8,128)(2,1)S(1)}, u32[]{:S(2)}, u32[]{:S(2)}) %collective-permute-start.12) | collective-permute-done | bytes 524320 | tf_op jit(solution)/shard_map/ppermute | solution.py:46
  391.2 5.3 multiply_convert_fusion.3
  396.5 21.5 %collective-permute-done.16 = bf16[128,2048]{0,1:T(8,128)(2,1)S(1)} collective-permute-done((bf16[128,2048]{0,1:T(8,128)(2,1)S(1)}, bf16[128,2048]{0,1:T(8,128)(2,1)S(1)}, u32[]{:S(2)}, u32[]{:S(2)}) %collective-permute-start.16) | collective-permute-done | bytes 524320 | tf_op jit(solution)/shard_map/ppermute | solution.py:46
  431.0 14.1 %collective-permute-done.28 = bf16[256,2048]{0,1:T(8,128)(2,1)S(1)} collective-permute-done((bf16[256,2048]{0,1:T(8,128)(2,1)S(1)}, bf16[256,2048]{0,1:T(8,128)(2,1)S(1)}, u32[]{:S(2)}, u32[]{:S(2)}) %collective-permute-start.28) | collective-permute-done | bytes 1048608 | tf_op jit(solution)/shard_map/ppermute | solution.py:42
  461.7 3.6 fusion.135
  485.7 5.5 convert_reduce_fusion
  491.2 3.7 convolution_convert_fusion.1
  495.0 6.0 fusion.140
  505.5 6.0 fusion.142
  515.6 3.7 convolution_convert_fusion.2
  519.3 10.4 collective-permute-done.66
  534.1 17.7 %collective-permute-done.76 = bf16[256,2048]{1,0:T(8,128)(2,1)} collective-permute-done((bf16[256,2048]{1,0:T(8,128)(2,1)}, bf16[256,2048]{1,0:T(8,128)(2,1)}, u32[]{:S(2)}, u32[]{:S(2)}) %collective-permute-start.76) | collective-permute-done | bytes 1048608 | tf_op jit(solution)/shard_map/ppermute | solution.py:42
  566.8 4.2 fusion.116
  578.8 6.8 convert_reduce_fusion.6
  585.7 8.9 multiply_reduce_fusion.1
  594.6 6.2 multiply_convert_fusion.1
  607.7 5.5 fusion.136
  619.9 4.1 reshape.1124
  624.0 12.5 %rev.76 = bf16[592,2,2,256]{3,2,1,0:T(2,128)(2,1)} reverse(bf16[592,2,2,256]{3,2,1,0:T(2,128)(2,1)} %reshape.1124), dimensions={2} | reverse | bytes 2424832 | tf_op jit(solution)/shard_map/rev | solution.py:36
  641.7 3.4 fusion.50
  645.4 11.9 collective-permute-done.57
  674.1 3.7 fusion.38
  695.7 3.8 collective-permute-done.47
  713.4 6.9 convert_reduce_fusion.1
  720.4 3.7 convolution_convert_fusion
  724.1 6.7 fusion.141
  736.7 5.7 fusion.143
  751.4 11.0 collective-permute-done.61
  768.3 15.9 %collective-permute-done.71 = bf16[256,2048]{1,0:T(8,128)(2,1)} collective-permute-done((bf16[256,2048]{1,0:T(8,128)(2,1)}, bf16[256,2048]{1,0:T(8,128)(2,1)}, u32[]{:S(2)}, u32[]{:S(2)}) %collective-permute-start.71) | collective-permute-done | bytes 1048608 | tf_op jit(solution)/shard_map/ppermute | solution.py:42
  805.7 6.6 convert_reduce_fusion.7
  812.3 9.1 multiply_reduce_fusion
  821.4 6.2 multiply_convert_fusion
  834.5 6.6 fusion.137
  863.2 8.2 collective-permute-done.54
  885.5 3.6 fusion.56
  891.6 13.4 %collective-permute-done.41 = bf16[256,1536]{1,0:T(8,128)(2,1)} collective-permute-done((bf16[256,1536]{1,0:T(8,128)(2,1)}, bf16[256,1536]{1,0:T(8,128)(2,1)}, u32[]{:S(2)}, u32[]{:S(2)}) %collective-permute-start.41) | collective-permute-done | bytes 786464 | tf_op jit(solution)/shard_map/ppermute | solution.py:42
  918.0 3.9 broadcast_select_fusion.5
  921.9 4.0 reshape.1125
  933.2 4.1 fusion.113
  946.5 3.4 reshape.1134
  949.9 8.2 rev.78
  975.1 40.2 %all-reduce.5.cloned.1.call-done = f32[20480]{0:T(1024)} async-done(((f32[20480]{0:T(1024)}), f32[20480]{0:T(1024)}) %all-reduce.5.cloned.1.call-update) | async-done | bytes 81936 | tf_op jit(solution)/shard_map/psum | solution.py:316
  1016.1 30.6 %reduce-scatter.21.cloned.1.call-done = bf16[1,256,1,512]{3,1,2,0:T(8,128)(2,1)} async-done(((bf16[4,256,1,512]{3,1,2,0:T(8,128)(2,1)}), bf16[1,256,1,512]{3,1,2,0:T(8,128)(2,1)}) %reduce-scatter.21.cloned.1.call-update) | async-done | bytes 262160 | tf_op jit(solution)/shard_map/reduce_scatter | solution.py:101
  1051.8 23.6 %reduce-scatter.17.cloned.1.call-done = bf16[1,256,1,512]{3,1,2,0:T(8,128)(2,1)} async-done(((bf16[4,256,1,512]{3,1,2,0:T(8,128)(2,1)}), bf16[1,256,1,512]{3,1,2,0:T(8,128)(2,1)}) %reduce-scatter.17.cloned.1.call-update) | async-done | bytes 262160 | tf_op jit(solution)/shard_map/reduce_scatter | solution.py:101
  1075.3 24.9 %reduce-scatter.9.cloned.1.call-done = bf16[1,256,3,128]{3,1,2,0:T(8,128)(2,1)} async-done(((bf16[4,256,3,128]{3,1,2,0:T(8,128)(2,1)}), bf16[1,256,3,128]{3,1,2,0:T(8,128)(2,1)}) %reduce-scatter.9.cloned.1.call-update) | async-done | bytes 196624 | tf_op jit(solution)/shard_map/reduce_scatter | solution.py:101
  1108.3 48.1 %all-gather.29.cloned.1.call-done = bf16[1280,1024]{1,0:T(8,128)(2,1)} async-done(((bf16[320,1024]{1,0:T(8,128)(2,1)}), bf16[1280,1024]{1,0:T(8,128)(2,1)}) %all-gather.29.cloned.1.call-update) | async-done | bytes 2621456 | tf_op jit(solution)/shard_map/all_gather | solution.py:289
  1159.3 52.1 %all-gather.27.cloned.1.call-done = bf16[1280,1024]{1,0:T(8,128)(2,1)} async-done(((bf16[320,1024]{1,0:T(8,128)(2,1)}), bf16[1280,1024]{1,0:T(8,128)(2,1)}) %all-gather.27.cloned.1.call-update) | async-done | bytes 2621456 | tf_op jit(solution)/shard_map/all_gather | solution.py:289
  (865 shorter events, 452.1 us)
Async XLA Ops:
  7.2 292.3 %all-gather.21.cloned.1.call-start = ((), (), s32[]{:S(2)}) async-start(), calls=%async_computation.18 | async-start | bytes 1310720 | tf_op jit(solution)/shard_map/all_gather | solution.py:91
  9.4 297.9 %all-gather.19.cloned.1.call-start = ((), (), s32[]{:S(2)}) async-start(), calls=%async_computation.17 | async-start | bytes 1310720 | tf_op jit(solution)/shard_map/all_gather | solution.py:91
  10.5 300.2 %all-gather.23.cloned.1.call-start = ((), (), s32[]{:S(2)}) async-start(), calls=%async_computation.19 | async-start | bytes 1310720 | tf_op jit(solution)/shard_map/all_gather | solution.py:91
  11.5 302.9 %all-gather.25.cloned.1.call-start = ((), (), s32[]{:S(2)}) async-start(), calls=%async_computation.20 | async-start | bytes 1310720 | tf_op jit(solution)/shard_map/all_gather | solution.py:91
  28.6 124.0 %collective-permute-start.24 = (bf16[256,512]{0,1:T(8,128)(2,1)S(1)}, bf16[256,512]{0,1:T(8,128)(2,1)}, u32[]{:S(2)}, u32[]{:S(2)}) collective-permute-start(bf16[256,512]{0,1:T(8,128)(2,1)S(1)} %bitcast.413), channel_id=1, source_target_pairs={{0,16},{16,0},{8,24},{24,8},{1,17},{17,1},{9,25},{25,9},{2,18},{18... | collective-permute-start | bytes 786440 | tf_op jit(solution)/shard_map/ppermute | solution.py:46
  30.3 132.3 %collective-permute-start.23 = (bf16[256,512]{0,1:T(8,128)(2,1)S(1)}, bf16[256,512]{0,1:T(8,128)(2,1)}, u32[]{:S(2)}, u32[]{:S(2)}) collective-permute-start(bf16[256,512]{0,1:T(8,128)(2,1)S(1)} %bitcast.414), channel_id=1, source_target_pairs={{0,8},{8,0},{16,24},{24,16},{1,9},{9,1},{17,25},{25,17},{2,10},{10... | collective-permute-start | bytes 786440 | tf_op jit(solution)/shard_map/ppermute | solution.py:42
  49.0 116.7 %collective-permute-start.6 = (bf16[256,512]{0,1:T(8,128)(2,1)S(1)}, bf16[256,512]{0,1:T(8,128)(2,1)}, u32[]{:S(2)}, u32[]{:S(2)}) collective-permute-start(bf16[256,512]{0,1:T(8,128)(2,1)S(1)} %bitcast.410), channel_id=1, source_target_pairs={{0,16},{16,0},{8,24},{24,8},{1,17},{17,1},{9,25},{25,9},{2,18},{18... | collective-permute-start | bytes 786440 | tf_op jit(solution)/shard_map/ppermute | solution.py:46
  49.6 119.0 %collective-permute-start.5 = (bf16[256,512]{0,1:T(8,128)(2,1)S(1)}, bf16[256,512]{0,1:T(8,128)(2,1)}, u32[]{:S(2)}, u32[]{:S(2)}) collective-permute-start(bf16[256,512]{0,1:T(8,128)(2,1)S(1)} %bitcast.411), channel_id=1, source_target_pairs={{0,8},{8,0},{16,24},{24,16},{1,9},{9,1},{17,25},{25,17},{2,10},{10... | collective-permute-start | bytes 786440 | tf_op jit(solution)/shard_map/ppermute | solution.py:42
  75.6 115.4 %collective-permute-start.20 = (bf16[256,1536]{0,1:T(8,128)(2,1)S(1)}, bf16[256,1536]{0,1:T(8,128)(2,1)}, u32[]{:S(2)}, u32[]{:S(2)}) collective-permute-start(bf16[256,1536]{0,1:T(8,128)(2,1)S(1)} %bitcast.384), channel_id=1, source_target_pairs={{0,16},{16,0},{8,24},{24,8},{1,17},{17,1},{9,25},{25,9},{2,18},{18... | collective-permute-start | bytes 2359304 | tf_op jit(solution)/shard_map/ppermute | solution.py:46
  77.8 889.3 %reduce-scatter.15.cloned.1.call-start = ((), (), s32[]{:S(2)}) async-start(), calls=%async_computation.12 | async-start | bytes 327680 | tf_op jit(solution)/shard_map/reduce_scatter | solution.py:101
  162.6 30.5 %collective-permute-start.19 = (bf16[256,1536]{0,1:T(8,128)(2,1)S(1)}, bf16[256,1536]{0,1:T(8,128)(2,1)S(1)}, u32[]{:S(2)}, u32[]{:S(2)}) collective-permute-start(bf16[256,1536]{0,1:T(8,128)(2,1)S(1)} %bitcast.386), channel_id=1, source_target_pairs={{0,8},{8,0},{16,24},{24,16},{1,9},{9,1},{17,25},{25,17},{2,10},{10... | collective-permute-start | bytes 2359304 | tf_op jit(solution)/shard_map/ppermute | solution.py:42
  165.6 29.0 %collective-permute-start.2 = (bf16[256,1536]{0,1:T(8,128)(2,1)S(1)}, bf16[256,1536]{0,1:T(8,128)(2,1)S(1)}, u32[]{:S(2)}, u32[]{:S(2)}) collective-permute-start(bf16[256,1536]{0,1:T(8,128)(2,1)S(1)} %bitcast.388), channel_id=1, source_target_pairs={{0,16},{16,0},{8,24},{24,8},{1,17},{17,1},{9,25},{25,9},{2,18},{18... | collective-permute-start | bytes 2359304 | tf_op jit(solution)/shard_map/ppermute | solution.py:46
  168.6 28.0 %collective-permute-start.1 = (bf16[256,1536]{0,1:T(8,128)(2,1)S(1)}, bf16[256,1536]{0,1:T(8,128)(2,1)S(1)}, u32[]{:S(2)}, u32[]{:S(2)}) collective-permute-start(bf16[256,1536]{0,1:T(8,128)(2,1)S(1)} %bitcast.389), channel_id=1, source_target_pairs={{0,8},{8,0},{16,24},{24,16},{1,9},{9,1},{17,25},{25,17},{2,10},{10... | collective-permute-start | bytes 2359304 | tf_op jit(solution)/shard_map/ppermute | solution.py:42
  190.3 24.2 %collective-permute-start = (bf16[2,320,1024]{2,1,0:T(8,128)(2,1)S(1)}, bf16[2,320,1024]{2,1,0:T(8,128)(2,1)S(1)}, u32[]{:S(2)}, u32[]{:S(2)}) collective-permute-start(bf16[2,320,1024]{2,1,0:T(8,128)(2,1)S(1)} %copy-done.63), channel_id=1, source_target_pairs={{0,4},{4,0},{1,5},{5,1},{2,6},{6,2},{3,7},{7,3},{8,12},{12,8},{9,1... | collective-permute-start | bytes 3932168 | tf_op jit(solution)/shard_map/ppermute | solution.py:50
  192.8 97.4 %collective-permute-start.22 = (bf16[128,1536]{0,1:T(8,128)(2,1)}, bf16[128,1536]{0,1:T(8,128)(2,1)S(1)}, u32[]{:S(2)}, u32[]{:S(2)}) collective-permute-start(bf16[128,1536]{0,1:T(8,128)(2,1)} %slice.877), channel_id=1, source_target_pairs={{0,8},{8,0},{16,24},{24,16},{1,9},{9,1},{17,25},{25,17},{2,10},{10... | collective-permute-start | bytes 1179656 | tf_op jit(solution)/shard_map/ppermute | solution.py:42
  290.2 31.6 %collective-permute-start.9 = (bf16[592,1024]{1,0:T(8,128)(2,1)}, bf16[592,1024]{1,0:T(8,128)(2,1)}, u32[]{:S(2)}, u32[]{:S(2)}) collective-permute-start(bf16[592,1024]{1,0:T(8,128)(2,1)} %convolution_convert_fusion.5), channel_id=1, source_target_pairs={{0,4},{4,0},{1,5},{5,1},{2,6},{6,2},{3,7},{7,3},{8,12},{12,8},{9,1... | collective-permute-start | bytes 3637256 | tf_op jit(solution)/shard_map/ppermute | solution.py:50
  302.3 60.2 %collective-permute-start.15 = (bf16[256,2048]{0,1:T(8,128)(2,1)}, bf16[256,2048]{0,1:T(8,128)(2,1)}, u32[]{:S(2)}, u32[]{:S(2)}) collective-permute-start(bf16[256,2048]{0,1:T(8,128)(2,1)} %bitcast.41), channel_id=1, source_target_pairs={{0,16},{16,0},{8,24},{24,8},{1,17},{17,1},{9,25},{25,9},{2,18},{18... | collective-permute-start | bytes 3145736 | tf_op jit(solution)/shard_map/ppermute | solution.py:46
  303.9 53.9 %collective-permute-start.14 = (bf16[256,2048]{0,1:T(8,128)(2,1)}, bf16[256,2048]{0,1:T(8,128)(2,1)}, u32[]{:S(2)}, u32[]{:S(2)}) collective-permute-start(bf16[256,2048]{0,1:T(8,128)(2,1)} %bitcast.41), channel_id=1, source_target_pairs={{0,8},{8,0},{16,24},{24,16},{1,9},{9,1},{17,25},{25,17},{2,10},{10... | collective-permute-start | bytes 3145736 | tf_op jit(solution)/shard_map/ppermute | solution.py:42
  310.5 49.1 %collective-permute-start.11 = (bf16[256,2048]{0,1:T(8,128)(2,1)}, bf16[256,2048]{0,1:T(8,128)(2,1)}, u32[]{:S(2)}, u32[]{:S(2)}) collective-permute-start(bf16[256,2048]{0,1:T(8,128)(2,1)} %bitcast.33), channel_id=1, source_target_pairs={{0,16},{16,0},{8,24},{24,8},{1,17},{17,1},{9,25},{25,9},{2,18},{18... | collective-permute-start | bytes 3145736 | tf_op jit(solution)/shard_map/ppermute | solution.py:46
  310.6 43.0 %collective-permute-start.10 = (bf16[256,2048]{0,1:T(8,128)(2,1)}, bf16[256,2048]{0,1:T(8,128)(2,1)}, u32[]{:S(2)}, u32[]{:S(2)}) collective-permute-start(bf16[256,2048]{0,1:T(8,128)(2,1)} %bitcast.33), channel_id=1, source_target_pairs={{0,8},{8,0},{16,24},{24,16},{1,9},{9,1},{17,25},{25,17},{2,10},{10... | collective-permute-start | bytes 3145736 | tf_op jit(solution)/shard_map/ppermute | solution.py:42
  321.8 102.9 %collective-permute-start.33 = (bf16[256,2048]{0,1:T(8,128)(2,1)S(1)}, bf16[256,2048]{0,1:T(8,128)(2,1)S(1)}, u32[]{:S(2)}, u32[]{:S(2)}) collective-permute-start(bf16[256,2048]{0,1:T(8,128)(2,1)S(1)} %bitcast.377), channel_id=1, source_target_pairs={{0,16},{16,0},{8,24},{24,8},{1,17},{17,1},{9,25},{25,9},{2,18},{18... | collective-permute-start | bytes 3145736 | tf_op jit(solution)/shard_map/ppermute | solution.py:46
  353.7 71.9 %collective-permute-start.32 = (bf16[256,2048]{0,1:T(8,128)(2,1)S(1)}, bf16[256,2048]{0,1:T(8,128)(2,1)S(1)}, u32[]{:S(2)}, u32[]{:S(2)}) collective-permute-start(bf16[256,2048]{0,1:T(8,128)(2,1)S(1)} %bitcast.378), channel_id=1, source_target_pairs={{0,8},{8,0},{16,24},{24,16},{1,9},{9,1},{17,25},{25,17},{2,10},{10... | collective-permute-start | bytes 3145736 | tf_op jit(solution)/shard_map/ppermute | solution.py:42
  357.8 26.8 %collective-permute-start.12 = (bf16[128,2048]{0,1:T(8,128)(2,1)S(1)}, bf16[128,2048]{0,1:T(8,128)(2,1)S(1)}, u32[]{:S(2)}, u32[]{:S(2)}) collective-permute-start(bf16[128,2048]{0,1:T(8,128)(2,1)S(1)} %slice.868), channel_id=1, source_target_pairs={{0,16},{16,0},{8,24},{24,8},{1,17},{17,1},{9,25},{25,9},{2,18},{18... | collective-permute-start | bytes 1572872 | tf_op jit(solution)/shard_map/ppermute | solution.py:46
  359.6 68.6 %collective-permute-start.29 = (bf16[256,2048]{0,1:T(8,128)(2,1)S(1)}, bf16[256,2048]{0,1:T(8,128)(2,1)S(1)}, u32[]{:S(2)}, u32[]{:S(2)}) collective-permute-start(bf16[256,2048]{0,1:T(8,128)(2,1)S(1)} %bitcast.374), channel_id=1, source_target_pairs={{0,16},{16,0},{8,24},{24,8},{1,17},{17,1},{9,25},{25,9},{2,18},{18... | collective-permute-start | bytes 3145736 | tf_op jit(solution)/shard_map/ppermute | solution.py:46
  362.5 28.5 %collective-permute-start.13 = (bf16[128,2048]{0,1:T(8,128)(2,1)S(1)}, bf16[128,2048]{0,1:T(8,128)(2,1)S(1)}, u32[]{:S(2)}, u32[]{:S(2)}) collective-permute-start(bf16[128,2048]{0,1:T(8,128)(2,1)S(1)} %slice.869), channel_id=1, source_target_pairs={{0,8},{8,0},{16,24},{24,16},{1,9},{9,1},{17,25},{25,17},{2,10},{10... | collective-permute-start | bytes 1572872 | tf_op jit(solution)/shard_map/ppermute | solution.py:42
  384.6 36.8 %collective-permute-start.17 = (bf16[128,2048]{0,1:T(8,128)(2,1)S(1)}, bf16[128,2048]{0,1:T(8,128)(2,1)S(1)}, u32[]{:S(2)}, u32[]{:S(2)}) collective-permute-start(bf16[128,2048]{0,1:T(8,128)(2,1)S(1)} %slice.872), channel_id=1, source_target_pairs={{0,8},{8,0},{16,24},{24,16},{1,9},{9,1},{17,25},{25,17},{2,10},{10... | collective-permute-start | bytes 1572872 | tf_op jit(solution)/shard_map/ppermute | solution.py:42
  390.9 27.0 %collective-permute-start.16 = (bf16[128,2048]{0,1:T(8,128)(2,1)S(1)}, bf16[128,2048]{0,1:T(8,128)(2,1)S(1)}, u32[]{:S(2)}, u32[]{:S(2)}) collective-permute-start(bf16[128,2048]{0,1:T(8,128)(2,1)S(1)} %slice.871), channel_id=1, source_target_pairs={{0,16},{16,0},{8,24},{24,8},{1,17},{17,1},{9,25},{25,9},{2,18},{18... | collective-permute-start | bytes 1572872 | tf_op jit(solution)/shard_map/ppermute | solution.py:46
  417.9 27.2 %collective-permute-start.28 = (bf16[256,2048]{0,1:T(8,128)(2,1)S(1)}, bf16[256,2048]{0,1:T(8,128)(2,1)S(1)}, u32[]{:S(2)}, u32[]{:S(2)}) collective-permute-start(bf16[256,2048]{0,1:T(8,128)(2,1)S(1)} %bitcast.375), channel_id=1, source_target_pairs={{0,8},{8,0},{16,24},{24,16},{1,9},{9,1},{17,25},{25,17},{2,10},{10... | collective-permute-start | bytes 3145736 | tf_op jit(solution)/shard_map/ppermute | solution.py:42
  425.5 51.7 %collective-permute-start.35 = (bf16[128,2048]{0,1:T(8,128)(2,1)}, bf16[128,2048]{0,1:T(8,128)(2,1)}, u32[]{:S(2)}, u32[]{:S(2)}) collective-permute-start(bf16[128,2048]{0,1:T(8,128)(2,1)} %slice.890), channel_id=1, source_target_pairs={{0,8},{8,0},{16,24},{24,16},{1,9},{9,1},{17,25},{25,17},{2,10},{10... | collective-permute-start | bytes 1572872 | tf_op jit(solution)/shard_map/ppermute | solution.py:42
  426.4 48.9 %collective-permute-start.34 = (bf16[128,2048]{0,1:T(8,128)(2,1)}, bf16[128,2048]{0,1:T(8,128)(2,1)}, u32[]{:S(2)}, u32[]{:S(2)}) collective-permute-start(bf16[128,2048]{0,1:T(8,128)(2,1)} %slice.889), channel_id=1, source_target_pairs={{0,16},{16,0},{8,24},{24,8},{1,17},{17,1},{9,25},{25,9},{2,18},{18... | collective-permute-start | bytes 1572872 | tf_op jit(solution)/shard_map/ppermute | solution.py:46
  429.0 51.4 %collective-permute-start.31 = (bf16[128,2048]{0,1:T(8,128)(2,1)}, bf16[128,2048]{0,1:T(8,128)(2,1)}, u32[]{:S(2)}, u32[]{:S(2)}) collective-permute-start(bf16[128,2048]{0,1:T(8,128)(2,1)} %slice.888), channel_id=1, source_target_pairs={{0,8},{8,0},{16,24},{24,16},{1,9},{9,1},{17,25},{25,17},{2,10},{10... | collective-permute-start | bytes 1572872 | tf_op jit(solution)/shard_map/ppermute | solution.py:42
  446.0 33.2 %collective-permute-start.30 = (bf16[128,2048]{0,1:T(8,128)(2,1)}, bf16[128,2048]{0,1:T(8,128)(2,1)}, u32[]{:S(2)}, u32[]{:S(2)}) collective-permute-start(bf16[128,2048]{0,1:T(8,128)(2,1)} %slice.887), channel_id=1, source_target_pairs={{0,16},{16,0},{8,24},{24,8},{1,17},{17,1},{9,25},{25,9},{2,18},{18... | collective-permute-start | bytes 1572872 | tf_op jit(solution)/shard_map/ppermute | solution.py:46
  500.9 63.1 %collective-permute-start.37 = (bf16[592,1024]{1,0:T(8,128)(2,1)}, bf16[592,1024]{1,0:T(8,128)(2,1)}, u32[]{:S(2)}, u32[]{:S(2)}) collective-permute-start(bf16[592,1024]{1,0:T(8,128)(2,1)} %convolution_convert_fusion.1), channel_id=1, source_target_pairs={{0,4},{4,0},{1,5},{5,1},{2,6},{6,2},{3,7},{7,3},{8,12},{12,8},{9,1... | collective-permute-start | bytes 3637256 | tf_op jit(solution)/shard_map/ppermute | solution.py:50
  502.1 55.8 %collective-permute-start.68 = (bf16[256,2048]{1,0:T(8,128)(2,1)}, bf16[256,2048]{1,0:T(8,128)(2,1)}, u32[]{:S(2)}, u32[]{:S(2)}) collective-permute-start(bf16[256,2048]{1,0:T(8,128)(2,1)} %pad_maximum_fusion.6), channel_id=1, source_target_pairs={{0,16},{16,0},{8,24},{24,8},{1,17},{17,1},{9,25},{25,9},{2,18},{18... | collective-permute-start | bytes 3145736 | tf_op jit(solution)/shard_map/ppermute | solution.py:46
  503.4 26.3 %collective-permute-start.66 = (bf16[256,2048]{1,0:T(8,128)(2,1)}, bf16[256,2048]{1,0:T(8,128)(2,1)}, u32[]{:S(2)}, u32[]{:S(2)}) collective-permute-start(bf16[256,2048]{1,0:T(8,128)(2,1)} %pad_maximum_fusion.5), channel_id=1, source_target_pairs={{0,8},{8,0},{16,24},{24,16},{1,9},{9,1},{17,25},{25,17},{2,10},{10... | collective-permute-start | bytes 3145736 | tf_op jit(solution)/shard_map/ppermute | solution.py:42
  512.8 48.4 %collective-permute-start.78 = (bf16[256,2048]{1,0:T(8,128)(2,1)}, bf16[256,2048]{1,0:T(8,128)(2,1)}, u32[]{:S(2)}, u32[]{:S(2)}) collective-permute-start(bf16[256,2048]{1,0:T(8,128)(2,1)} %pad_maximum_fusion.10), channel_id=1, source_target_pairs={{0,16},{16,0},{8,24},{24,8},{1,17},{17,1},{9,25},{25,9},{2,18},{18... | collective-permute-start | bytes 3145736 | tf_op jit(solution)/shard_map/ppermute | solution.py:46
  515.6 36.3 %collective-permute-start.76 = (bf16[256,2048]{1,0:T(8,128)(2,1)}, bf16[256,2048]{1,0:T(8,128)(2,1)}, u32[]{:S(2)}, u32[]{:S(2)}) collective-permute-start(bf16[256,2048]{1,0:T(8,128)(2,1)} %pad_maximum_fusion.9), channel_id=1, source_target_pairs={{0,8},{8,0},{16,24},{24,16},{1,9},{9,1},{17,25},{25,17},{2,10},{10... | collective-permute-start | bytes 3145736 | tf_op jit(solution)/shard_map/ppermute | solution.py:42
  529.7 37.1 %collective-permute-start.36 = (bf16[592,1024]{1,0:T(8,128)(2,1)}, bf16[592,1024]{1,0:T(8,128)(2,1)S(1)}, u32[]{:S(2)}, u32[]{:S(2)}) collective-permute-start(bf16[592,1024]{1,0:T(8,128)(2,1)} %convolution_convert_fusion.2), channel_id=1, source_target_pairs={{0,4},{4,0},{1,5},{5,1},{2,6},{6,2},{3,7},{7,3},{8,12},{12,8},{9,1... | collective-permute-start | bytes 3637256 | tf_op jit(solution)/shard_map/ppermute | solution.py:50
  551.8 89.8 %collective-permute-start.67 = (bf16[128,2048]{1,0:T(8,128)(2,1)}, bf16[128,2048]{1,0:T(8,128)(2,1)}, u32[]{:S(2)}, u32[]{:S(2)}) collective-permute-start(bf16[128,2048]{1,0:T(8,128)(2,1)} %fusion.48), channel_id=1, source_target_pairs={{0,16},{16,0},{8,24},{24,8},{1,17},{17,1},{9,25},{25,9},{2,18},{18... | collective-permute-start | bytes 1572872 | tf_op jit(solution)/shard_map/ppermute | solution.py:46
  558.0 116.2 %collective-permute-start.77 = (bf16[128,2048]{1,0:T(8,128)(2,1)}, bf16[128,2048]{1,0:T(8,128)(2,1)}, u32[]{:S(2)}, u32[]{:S(2)}) collective-permute-start(bf16[128,2048]{1,0:T(8,128)(2,1)} %fusion.36), channel_id=1, source_target_pairs={{0,16},{16,0},{8,24},{24,8},{1,17},{17,1},{9,25},{25,9},{2,18},{18... | collective-permute-start | bytes 1572872 | tf_op jit(solution)/shard_map/ppermute | solution.py:46
  614.1 26.6 %collective-permute-start.58 = (bf16[256,512]{0,1:T(8,128)(2,1)}, bf16[256,512]{0,1:T(8,128)(2,1)}, u32[]{:S(2)}, u32[]{:S(2)}) collective-permute-start(bf16[256,512]{0,1:T(8,128)(2,1)} %pad_maximum_fusion.22), channel_id=1, source_target_pairs={{0,16},{16,0},{8,24},{24,8},{1,17},{17,1},{9,25},{25,9},{2,18},{18... | collective-permute-start | bytes 786440 | tf_op jit(solution)/shard_map/ppermute | solution.py:46
  636.5 51.5 %collective-permute-start.48 = (bf16[256,1536]{1,0:T(8,128)(2,1)}, bf16[256,1536]{1,0:T(8,128)(2,1)}, u32[]{:S(2)}, u32[]{:S(2)}) collective-permute-start(bf16[256,1536]{1,0:T(8,128)(2,1)} %pad_maximum_fusion.18), channel_id=1, source_target_pairs={{0,16},{16,0},{8,24},{24,8},{1,17},{17,1},{9,25},{25,9},{2,18},{18... | collective-permute-start | bytes 2359304 | tf_op jit(solution)/shard_map/ppermute | solution.py:46
  668.7 298.6 %reduce-scatter.19.cloned.1.call-start = ((), (), s32[]{:S(2)}) async-start(), calls=%async_computation.14 | async-start | bytes 1310720 | tf_op jit(solution)/shard_map/reduce_scatter | solution.py:101
  674.1 293.7 %reduce-scatter.23.cloned.1.call-start = ((), (), s32[]{:S(2)}) async-start(), calls=%async_computation.16 | async-start | bytes 1310720 | tf_op jit(solution)/shard_map/reduce_scatter | solution.py:101
  695.6 274.0 %reduce-scatter.11.cloned.1.call-start = ((), (), s32[]{:S(2)}) async-start(), calls=%async_computation.9 | async-start | bytes 983040 | tf_op jit(solution)/shard_map/reduce_scatter | solution.py:101
  703.4 42.9 %collective-permute-start.49 = (bf16[128,1536]{1,0:T(8,128)(2,1)}, bf16[128,1536]{1,0:T(8,128)(2,1)S(1)}, u32[]{:S(2)}, u32[]{:S(2)}) collective-permute-start(bf16[128,1536]{1,0:T(8,128)(2,1)} %get-tuple-element.109), channel_id=1, source_target_pairs={{0,8},{8,0},{16,24},{24,16},{1,9},{9,1},{17,25},{25,17},{2,10},{10... | collective-permute-start | bytes 1179656 | tf_op jit(solution)/shard_map/ppermute | solution.py:42
  731.8 64.0 %collective-permute-start.39 = (bf16[592,1024]{1,0:T(8,128)(2,1)}, bf16[592,1024]{1,0:T(8,128)(2,1)}, u32[]{:S(2)}, u32[]{:S(2)}) collective-permute-start(bf16[592,1024]{1,0:T(8,128)(2,1)} %convolution_convert_fusion), channel_id=1, source_target_pairs={{0,4},{4,0},{1,5},{5,1},{2,6},{6,2},{3,7},{7,3},{8,12},{12,8},{9,1... | collective-permute-start | bytes 3637256 | tf_op jit(solution)/shard_map/ppermute | solution.py:50
  734.6 55.5 %collective-permute-start.63 = (bf16[256,2048]{1,0:T(8,128)(2,1)}, bf16[256,2048]{1,0:T(8,128)(2,1)}, u32[]{:S(2)}, u32[]{:S(2)}) collective-permute-start(bf16[256,2048]{1,0:T(8,128)(2,1)} %pad_maximum_fusion.4), channel_id=1, source_target_pairs={{0,16},{16,0},{8,24},{24,8},{1,17},{17,1},{9,25},{25,9},{2,18},{18... | collective-permute-start | bytes 3145736 | tf_op jit(solution)/shard_map/ppermute | solution.py:46
  736.1 26.3 %collective-permute-start.61 = (bf16[256,2048]{1,0:T(8,128)(2,1)}, bf16[256,2048]{1,0:T(8,128)(2,1)}, u32[]{:S(2)}, u32[]{:S(2)}) collective-permute-start(bf16[256,2048]{1,0:T(8,128)(2,1)} %pad_maximum_fusion.3), channel_id=1, source_target_pairs={{0,8},{8,0},{16,24},{24,16},{1,9},{9,1},{17,25},{25,17},{2,10},{10... | collective-permute-start | bytes 3145736 | tf_op jit(solution)/shard_map/ppermute | solution.py:42
  743.7 49.1 %collective-permute-start.73 = (bf16[256,2048]{1,0:T(8,128)(2,1)}, bf16[256,2048]{1,0:T(8,128)(2,1)}, u32[]{:S(2)}, u32[]{:S(2)}) collective-permute-start(bf16[256,2048]{1,0:T(8,128)(2,1)} %pad_maximum_fusion.8), channel_id=1, source_target_pairs={{0,16},{16,0},{8,24},{24,8},{1,17},{17,1},{9,25},{25,9},{2,18},{18... | collective-permute-start | bytes 3145736 | tf_op jit(solution)/shard_map/ppermute | solution.py:46
  746.3 37.8 %collective-permute-start.71 = (bf16[256,2048]{1,0:T(8,128)(2,1)}, bf16[256,2048]{1,0:T(8,128)(2,1)}, u32[]{:S(2)}, u32[]{:S(2)}) collective-permute-start(bf16[256,2048]{1,0:T(8,128)(2,1)} %pad_maximum_fusion.7), channel_id=1, source_target_pairs={{0,8},{8,0},{16,24},{24,16},{1,9},{9,1},{17,25},{25,17},{2,10},{10... | collective-permute-start | bytes 3145736 | tf_op jit(solution)/shard_map/ppermute | solution.py:42
  751.1 220.7 %reduce-scatter.13.cloned.1.call-start = ((), (), s32[]{:S(2)}) async-start(), calls=%async_computation.11 | async-start | bytes 327680 | tf_op jit(solution)/shard_map/reduce_scatter | solution.py:101
  766.8 118.7 %collective-permute-start.62 = (bf16[128,2048]{1,0:T(8,128)(2,1)}, bf16[128,2048]{1,0:T(8,128)(2,1)}, u32[]{:S(2)}, u32[]{:S(2)}) collective-permute-start(bf16[128,2048]{1,0:T(8,128)(2,1)} %fusion.54), channel_id=1, source_target_pairs={{0,16},{16,0},{8,24},{24,8},{1,17},{17,1},{9,25},{25,9},{2,18},{18... | collective-permute-start | bytes 1572872 | tf_op jit(solution)/shard_map/ppermute | solution.py:46
  788.5 64.8 %collective-permute-start.72 = (bf16[128,2048]{1,0:T(8,128)(2,1)}, bf16[128,2048]{1,0:T(8,128)(2,1)}, u32[]{:S(2)}, u32[]{:S(2)}) collective-permute-start(bf16[128,2048]{1,0:T(8,128)(2,1)} %fusion.42), channel_id=1, source_target_pairs={{0,16},{16,0},{8,24},{24,8},{1,17},{17,1},{9,25},{25,9},{2,18},{18... | collective-permute-start | bytes 1572872 | tf_op jit(solution)/shard_map/ppermute | solution.py:46
  845.7 31.1 %collective-permute-start.40 = (bf16[592,1024]{1,0:T(8,128)(2,1)}, bf16[592,1024]{1,0:T(8,128)(2,1)}, u32[]{:S(2)}, u32[]{:S(2)}) collective-permute-start(bf16[592,1024]{1,0:T(8,128)(2,1)} %convolution_convert_fusion.6), channel_id=1, source_target_pairs={{0,4},{4,0},{1,5},{5,1},{2,6},{6,2},{3,7},{7,3},{8,12},{12,8},{9,1... | collective-permute-start | bytes 3637256 | tf_op jit(solution)/shard_map/ppermute | solution.py:50
  874.1 141.1 %all-reduce.5.cloned.1.call-start = ((), (), s32[]{:S(2)}) async-start(), calls=%async_computation.10 | async-start | bytes 163840 | tf_op jit(solution)/shard_map/psum | solution.py:316
  880.8 165.8 %reduce-scatter.21.cloned.1.call-start = ((), (), s32[]{:S(2)}) async-start(), calls=%async_computation.15 | async-start | bytes 1310720 | tf_op jit(solution)/shard_map/reduce_scatter | solution.py:101
  882.0 193.3 %reduce-scatter.17.cloned.1.call-start = ((), (), s32[]{:S(2)}) async-start(), calls=%async_computation.13 | async-start | bytes 1310720 | tf_op jit(solution)/shard_map/reduce_scatter | solution.py:101
  890.7 35.2 %collective-permute-start.43 = (bf16[256,1536]{1,0:T(8,128)(2,1)}, bf16[256,1536]{1,0:T(8,128)(2,1)}, u32[]{:S(2)}, u32[]{:S(2)}) collective-permute-start(bf16[256,1536]{1,0:T(8,128)(2,1)} %pad_maximum_fusion.16), channel_id=1, source_target_pairs={{0,16},{16,0},{8,24},{24,8},{1,17},{17,1},{9,25},{25,9},{2,18},{18... | collective-permute-start | bytes 2359304 | tf_op jit(solution)/shard_map/ppermute | solution.py:46
  917.9 182.3 %reduce-scatter.9.cloned.1.call-start = ((), (), s32[]{:S(2)}) async-start(), calls=%async_computation.8 | async-start | bytes 983040 | tf_op jit(solution)/shard_map/reduce_scatter | solution.py:101
  943.2 213.1 %all-gather.29.cloned.1.call-start = ((), (), s32[]{:S(2)}) async-start(), calls=%async_computation.22 | async-start | bytes 3276800 | tf_op jit(solution)/shard_map/all_gather | solution.py:289
  966.5 244.8 %all-gather.27.cloned.1.call-start = ((), (), s32[]{:S(2)}) async-start(), calls=%async_computation.21 | async-start | bytes 3276800 | tf_op jit(solution)/shard_map/all_gather | solution.py:289
  1046.7 53.5 %collective-permute-start.75 = (bf16[256,1,512]{2,0,1:T(8,128)(2,1)}, bf16[256,1,512]{2,0,1:T(8,128)(2,1)S(1)}, u32[]{:S(2)}, u32[]{:S(2)}) collective-permute-start(bf16[256,1,512]{2,0,1:T(8,128)(2,1)} %bitcast.440), channel_id=1, source_target_pairs={{0,4},{4,0},{1,5},{5,1},{2,6},{6,2},{3,7},{7,3},{8,12},{12,8},{9,1... | collective-permute-start | bytes 786440 | tf_op jit(solution)/shard_map/ppermute | solution.py:50
  1075.3 26.2 %collective-permute-start.65 = (bf16[256,1,512]{2,0,1:T(8,128)(2,1)}, bf16[256,1,512]{2,0,1:T(8,128)(2,1)}, u32[]{:S(2)}, u32[]{:S(2)}) collective-permute-start(bf16[256,1,512]{2,0,1:T(8,128)(2,1)} %bitcast.441), channel_id=1, source_target_pairs={{0,4},{4,0},{1,5},{5,1},{2,6},{6,2},{3,7},{7,3},{8,12},{12,8},{9,1... | collective-permute-start | bytes 786440 | tf_op jit(solution)/shard_map/ppermute | solution.py:50
  (165 other events, 1921.1 us)
Sparse Core Ops, SparseCore 0:
  10.2 36.8 all-gather.20
  49.2 35.7 all-gather.18
  87.1 36.1 all-gather.22
  124.8 30.8 all-gather.24
  668.8 16.7 reduce-scatter.14
  687.8 25.4 reduce-scatter.18
  715.6 25.8 reduce-scatter.22
  751.3 20.4 reduce-scatter.10
  874.3 17.6 reduce-scatter.12
  897.4 117.8 all-reduce.4
  1017.6 29.0 reduce-scatter.20
  1049.5 25.7 reduce-scatter.16
  1078.2 21.9 reduce-scatter.8
  1102.2 54.0 all-gather.28
  1157.7 53.5 all-gather.26
where the time goes:
time: 1230 us; the launch traced here: 1220 us
  waiting for transfers between devices  424 us (34%)
  local copies, waits for them, and re-layouts  235 us (19%)
  other arithmetic  203 us (17%)
  matrix products  144 us (12%)
  blocking collectives  117 us (10%)
  starting transfers between devices  77.4 us (6%)
  between operations  20.5 us (2%)
    ppermute x32, waiting for transfers between devices, send_x(): return lax.ppermute(values, 'fsdp', X_PAIRS)  133 us
    all_gather x2, waiting for transfers between devices, give_back(): return lax.all_gather(mine, 'tp', axis=0)[:slots]  100 us
    reduce_scatter x8, waiting for transfers between devices, scatter_matrix(): own = lax.psum_scatter(kept, 'tp', scatter_dimension=0, tiled=False)  79.1 us
    all_gather x4, blocking collectives, gather_matrix(): along = lax.all_gather(half, 'tp', axis=0)  77.4 us
    ppermute x32, waiting for transfers between devices, send_y(): return lax.ppermute(values, 'fsdp', Y_PAIRS)  70.2 us
    unnamed x340, local copies, waits for them, and re-layouts  62.1 us
    dot_general x8, matrix products, mm_tn(): lax.dot_general(left, right, (((0,), (0,)), ((), ())), preferred_element_...  41.5 us
    rev x11, local copies, waits for them, and re-layouts, reorder(): blocks = jnp.where(place % 2 == 1, blocks[..., :, ::-1, :], blocks)  40.8 us
  transfers between devices with their start and end apart: 96, of which 30 were waited for; matrix products, arithmetic and copies ran while one was open for 44% of the time, Pallas kernels for 0%

commit v1 on v0

--- a/solution.py
+++ b/solution.py
@@ -313,7 +313,9 @@
         from_core(jnp.stack([member(0), member(1)], axis=1), 2),
         from_core(member(3)[:, None], 1),
     ] + [reorder(member(k)) * first for k in (2, 4, 5, 6)]
-    summed = lax.psum(jnp.concatenate([a.reshape(-1) for a in joined]), ("fsdp", "ctx", "tp"))
+    summed = lax.psum(
+        lax.psum(jnp.concatenate([a.reshape(-1) for a in joined]), ("ctx", "tp")), "fsdp"
+    )
     whole, start = ([], 0)
     for a in joined:
         whole.append(summed[start : start + a.size])

time: 1230 us -> 1170 us (0.951)
  waiting for transfers between devices: 424 us -> 351 us
    psum x1 -> x2, waiting for transfers between devices: 40.2 us -> 0.01 us  [the longest x1 0.01 us: shards(): lax.psum(jnp.concatenate([a.reshape(-1) for a in joined]), ('ctx', 'tp'))]
    reduce_scatter x8, waiting for transfers between devices: 79.1 us -> 46 us  [scatter_matrix(): own = lax.psum_scatter(kept, 'tp', scatter_dimension=0, tiled=False)]
    concatenate x24, local copies, waits for them, and re-layouts: 12.8 us -> 27.4 us  [scatter_rows(): return jnp.concatenate([own_a, own_b])]
    unnamed x340 -> x336, local copies, waits for them, and re-layouts: 62.1 us -> 61.5 us
  transfers between devices with their start and end apart: 96 -> 97, of which waited for: 30 -> 29; matrix products, arithmetic and copies ran while one was open for 44% -> 47% of each run, Pallas kernels for 0% -> 0%
where the time goes in v1:
time: 1170 us; the launch traced here: 1150 us
  waiting for transfers between devices  351 us (30%)
  local copies, waits for them, and re-layouts  243 us (21%)
  other arithmetic  200 us (17%)
  matrix products  148 us (13%)
  blocking collectives  117 us (10%)
  starting transfers between devices  75.8 us (6%)
  between operations  20.5 us (2%)
    ppermute x32, waiting for transfers between devices, send_x(): return lax.ppermute(values, 'fsdp', X_PAIRS)  126 us
    all_gather x2, waiting for transfers between devices, give_back(): return lax.all_gather(mine, 'tp', axis=0)[:slots]  100 us
    all_gather x4, blocking collectives, gather_matrix(): along = lax.all_gather(half, 'tp', axis=0)  77.5 us
    ppermute x32, waiting for transfers between devices, send_y(): return lax.ppermute(values, 'fsdp', Y_PAIRS)  72.4 us
    unnamed x336, local copies, waits for them, and re-layouts  61.5 us
    reduce_scatter x8, waiting for transfers between devices, scatter_matrix(): own = lax.psum_scatter(kept, 'tp', scatter_dimension=0, tiled=False)  46 us
    dot_general x8, matrix products, mm_tn(): lax.dot_general(left, right, (((0,), (0,)), ((), ())), preferred_element_...  42.3 us
    rev x11, local copies, waits for them, and re-layouts, reorder(): blocks = jnp.where(place % 2 == 1, blocks[..., :, ::-1, :], blocks)  41.5 us
  transfers between devices with their start and end apart: 97, of which 29 were waited for; matrix products, arithmetic and copies ran while one was open for 47% of the time, Pallas kernels for 0%

profile of v1, /device:TPU:0, one launch (start us, length us, event | category | flops | bytes accessed | tf_op | source)
XLA Modules:
  0.0 1154.7 jit_solution(17108782257517651567)
XLA Ops:
  11.6 16.6 %all-gather.6 = bf16[1024,1,1,128]{0,3,2,1:T(8,128)(2,1)S(1)} all-gather(bf16[256,1,1,128]{0,3,2,1:T(8,128)(2,1)S(1)} %constant_dynamic-slice_fusion.8), channel_id=8, replica_groups=mesh['fsdp'=4,'ctx'=2,'tp'=4] {'tp'}, dimensions={0}, use_global_device_ids=true | all-gather | bytes 327680 | tf_op jit(solution)/shard_map/all_gather | solution.py:91
  31.9 16.8 %all-gather.2 = bf16[1024,1,1,128]{0,3,2,1:T(8,128)(2,1)S(1)} all-gather(bf16[256,1,1,128]{0,3,2,1:T(8,128)(2,1)S(1)} %constant_dynamic-slice_fusion.12), channel_id=4, replica_groups=mesh['fsdp'=4,'ctx'=2,'tp'=4] {'tp'}, dimensions={0}, use_global_device_ids=true | all-gather | bytes 327680 | tf_op jit(solution)/shard_map/all_gather | solution.py:91
  50.7 24.3 %all-gather.5 = bf16[1024,3,1,128]{0,3,2,1:T(8,128)(2,1)S(1)} all-gather(bf16[256,3,1,128]{0,3,2,1:T(8,128)(2,1)S(1)} %constant_dynamic-slice_fusion.9), channel_id=7, replica_groups=mesh['fsdp'=4,'ctx'=2,'tp'=4] {'tp'}, dimensions={0}, use_global_device_ids=true | all-gather | bytes 983040 | tf_op jit(solution)/shard_map/all_gather | solution.py:91
  80.6 39.9 %all-gather.11 = bf16[16,1,2816]{2,1,0:T(2,128)(2,1)S(1)} all-gather(bf16[1,1,2816]{2,1,0:T(2,128)(2,1)S(1)} %reshape.1168), channel_id=2, replica_groups=mesh['fsdp'=4,'ctx'=2,'tp'=4] {'fsdp','tp'}, dimensions={0}, use_global_device_ids=true | all-gather | bytes 95744 | tf_op jit(solution)/shard_map/all_gather | solution.py:236
  126.1 19.8 %all-gather.1 = bf16[1024,3,1,128]{0,3,2,1:T(8,128)(2,1)S(1)} all-gather(bf16[256,3,1,128]{0,3,2,1:T(8,128)(2,1)S(1)} %constant_dynamic-slice_fusion.13), channel_id=3, replica_groups=mesh['fsdp'=4,'ctx'=2,'tp'=4] {'tp'}, dimensions={0}, use_global_device_ids=true | all-gather | bytes 983040 | tf_op jit(solution)/shard_map/all_gather | solution.py:91
  173.8 6.2 collective-permute-done.25
  206.1 6.9 collective-permute-done.3
  216.2 9.2 dynamic_update_slice.3
  227.1 5.7 reshape.1095
  232.8 19.3 %rev.66 = bf16[2,592,2,2,256]{4,3,2,1,0:T(2,128)(2,1)} reverse(bf16[2,592,2,2,256]{4,3,2,1,0:T(2,128)(2,1)S(1)} %reshape.1095), dimensions={3} | reverse | bytes 4849664 | tf_op jit(solution)/shard_map/rev | solution.py:36
  257.1 5.0 fusion.120
  262.2 3.7 squeeze.95
  266.4 4.5 fusion.106
  277.9 3.6 fusion.134
  291.1 4.3 squeeze.100
  303.9 3.4 collective-permute-start.14
  326.2 27.4 %collective-permute-done.10 = bf16[256,2048]{0,1:T(8,128)(2,1)} collective-permute-done((bf16[256,2048]{0,1:T(8,128)(2,1)}, bf16[256,2048]{0,1:T(8,128)(2,1)}, u32[]{:S(2)}, u32[]{:S(2)}) %collective-permute-start.10) | collective-permute-done | bytes 1048608 | tf_op jit(solution)/shard_map/ppermute | solution.py:42
  367.7 17.0 %collective-permute-done.12 = bf16[128,2048]{0,1:T(8,128)(2,1)S(1)} collective-permute-done((bf16[128,2048]{0,1:T(8,128)(2,1)S(1)}, bf16[128,2048]{0,1:T(8,128)(2,1)S(1)}, u32[]{:S(2)}, u32[]{:S(2)}) %collective-permute-start.12) | collective-permute-done | bytes 524320 | tf_op jit(solution)/shard_map/ppermute | solution.py:46
  391.2 5.3 multiply_convert_fusion.3
  396.4 21.6 %collective-permute-done.16 = bf16[128,2048]{0,1:T(8,128)(2,1)S(1)} collective-permute-done((bf16[128,2048]{0,1:T(8,128)(2,1)S(1)}, bf16[128,2048]{0,1:T(8,128)(2,1)S(1)}, u32[]{:S(2)}, u32[]{:S(2)}) %collective-permute-start.16) | collective-permute-done | bytes 524320 | tf_op jit(solution)/shard_map/ppermute | solution.py:46
  431.0 14.2 %collective-permute-done.28 = bf16[256,2048]{0,1:T(8,128)(2,1)S(1)} collective-permute-done((bf16[256,2048]{0,1:T(8,128)(2,1)S(1)}, bf16[256,2048]{0,1:T(8,128)(2,1)S(1)}, u32[]{:S(2)}, u32[]{:S(2)}) %collective-permute-start.28) | collective-permute-done | bytes 1048608 | tf_op jit(solution)/shard_map/ppermute | solution.py:42
  461.5 3.6 fusion.135
  485.8 5.5 convert_reduce_fusion
  491.3 3.7 convolution_convert_fusion.1
  495.1 6.0 fusion.140
  505.6 5.9 fusion.142
  515.6 3.7 convolution_convert_fusion.2
  519.4 10.5 collective-permute-done.66
  534.2 17.8 %collective-permute-done.76 = bf16[256,2048]{1,0:T(8,128)(2,1)} collective-permute-done((bf16[256,2048]{1,0:T(8,128)(2,1)}, bf16[256,2048]{1,0:T(8,128)(2,1)}, u32[]{:S(2)}, u32[]{:S(2)}) %collective-permute-start.76) | collective-permute-done | bytes 1048608 | tf_op jit(solution)/shard_map/ppermute | solution.py:42
  566.9 4.2 fusion.116
  578.9 6.8 convert_reduce_fusion.6
  585.7 8.7 multiply_reduce_fusion.1
  594.5 6.2 multiply_convert_fusion.1
  607.6 5.5 fusion.136
  619.2 4.1 reshape.1124
  623.3 12.8 %rev.76 = bf16[592,2,2,256]{3,2,1,0:T(2,128)(2,1)} reverse(bf16[592,2,2,256]{3,2,1,0:T(2,128)(2,1)} %reshape.1124), dimensions={2} | reverse | bytes 2424832 | tf_op jit(solution)/shard_map/rev | solution.py:36
  643.8 3.4 fusion.50
  651.4 8.8 collective-permute-done.57
  672.3 6.7 convert_reduce_fusion.1
  679.1 3.7 convolution_convert_fusion
  695.0 7.4 convert_reduce_fusion.7
  702.4 8.5 multiply_reduce_fusion
  711.0 6.1 multiply_convert_fusion
  721.8 5.5 convolution_convert_fusion.6
  743.1 3.9 fusion.38
  776.0 9.5 fusion.141
  789.5 6.1 fusion.143
  805.5 10.1 collective-permute-done.61
  820.6 15.5 %collective-permute-done.71 = bf16[256,2048]{1,0:T(8,128)(2,1)} collective-permute-done((bf16[256,2048]{1,0:T(8,128)(2,1)}, bf16[256,2048]{1,0:T(8,128)(2,1)}, u32[]{:S(2)}, u32[]{:S(2)}) %collective-permute-start.71) | collective-permute-done | bytes 1048608 | tf_op jit(solution)/shard_map/ppermute | solution.py:42
  847.1 5.6 fusion.137
  854.2 8.9 collective-permute-done.53
  872.5 7.5 collective-permute-done.54
  892.8 3.6 fusion.56
  900.9 12.1 %collective-permute-done.41 = bf16[256,1536]{1,0:T(8,128)(2,1)} collective-permute-done((bf16[256,1536]{1,0:T(8,128)(2,1)}, bf16[256,1536]{1,0:T(8,128)(2,1)}, u32[]{:S(2)}, u32[]{:S(2)}) %collective-permute-start.41) | collective-permute-done | bytes 786464 | tf_op jit(solution)/shard_map/ppermute | solution.py:42
  924.7 3.9 broadcast_select_fusion.5
  928.6 4.0 reshape.1125
  938.4 4.1 fusion.113
  942.5 3.7 collective-permute-done.44
  953.0 3.4 reshape.1134
  956.4 8.2 rev.78
  987.9 21.2 %reduce-scatter.17.cloned.1.call-done = bf16[1,256,1,512]{3,1,2,0:T(8,128)(2,1)} async-done(((bf16[4,256,1,512]{3,1,2,0:T(8,128)(2,1)}), bf16[1,256,1,512]{3,1,2,0:T(8,128)(2,1)}) %reduce-scatter.17.cloned.1.call-update) | async-done | bytes 262160 | tf_op jit(solution)/shard_map/reduce_scatter | solution.py:101
  1009.1 24.7 %reduce-scatter.9.cloned.1.call-done = bf16[1,256,3,128]{3,1,2,0:T(8,128)(2,1)} async-done(((bf16[4,256,3,128]{3,1,2,0:T(8,128)(2,1)}), bf16[1,256,3,128]{3,1,2,0:T(8,128)(2,1)}) %reduce-scatter.9.cloned.1.call-update) | async-done | bytes 196624 | tf_op jit(solution)/shard_map/reduce_scatter | solution.py:101
  1041.9 48.1 %all-gather.29.cloned.1.call-done = bf16[1280,1024]{1,0:T(8,128)(2,1)} async-done(((bf16[320,1024]{1,0:T(8,128)(2,1)}), bf16[1280,1024]{1,0:T(8,128)(2,1)}) %all-gather.29.cloned.1.call-update) | async-done | bytes 2621456 | tf_op jit(solution)/shard_map/all_gather | solution.py:289
  1092.9 52.1 %all-gather.27.cloned.1.call-done = bf16[1280,1024]{1,0:T(8,128)(2,1)} async-done(((bf16[320,1024]{1,0:T(8,128)(2,1)}), bf16[1280,1024]{1,0:T(8,128)(2,1)}) %all-gather.27.cloned.1.call-update) | async-done | bytes 2621456 | tf_op jit(solution)/shard_map/all_gather | solution.py:289
  (864 shorter events, 448.0 us)
Async XLA Ops:
  7.2 292.4 %all-gather.21.cloned.1.call-start = ((), (), s32[]{:S(2)}) async-start(), calls=%async_computation.19 | async-start | bytes 1310720 | tf_op jit(solution)/shard_map/all_gather | solution.py:91
  9.4 297.9 %all-gather.19.cloned.1.call-start = ((), (), s32[]{:S(2)}) async-start(), calls=%async_computation.18 | async-start | bytes 1310720 | tf_op jit(solution)/shard_map/all_gather | solution.py:91
  10.5 300.0 %all-gather.23.cloned.1.call-start = ((), (), s32[]{:S(2)}) async-start(), calls=%async_computation.20 | async-start | bytes 1310720 | tf_op jit(solution)/shard_map/all_gather | solution.py:91
  11.5 302.7 %all-gather.25.cloned.1.call-start = ((), (), s32[]{:S(2)}) async-start(), calls=%async_computation.21 | async-start | bytes 1310720 | tf_op jit(solution)/shard_map/all_gather | solution.py:91
  28.6 124.0 %collective-permute-start.24 = (bf16[256,512]{0,1:T(8,128)(2,1)S(1)}, bf16[256,512]{0,1:T(8,128)(2,1)}, u32[]{:S(2)}, u32[]{:S(2)}) collective-permute-start(bf16[256,512]{0,1:T(8,128)(2,1)S(1)} %bitcast.413), channel_id=1, source_target_pairs={{0,16},{16,0},{8,24},{24,8},{1,17},{17,1},{9,25},{25,9},{2,18},{18... | collective-permute-start | bytes 786440 | tf_op jit(solution)/shard_map/ppermute | solution.py:46
  30.3 132.4 %collective-permute-start.23 = (bf16[256,512]{0,1:T(8,128)(2,1)S(1)}, bf16[256,512]{0,1:T(8,128)(2,1)}, u32[]{:S(2)}, u32[]{:S(2)}) collective-permute-start(bf16[256,512]{0,1:T(8,128)(2,1)S(1)} %bitcast.414), channel_id=1, source_target_pairs={{0,8},{8,0},{16,24},{24,16},{1,9},{9,1},{17,25},{25,17},{2,10},{10... | collective-permute-start | bytes 786440 | tf_op jit(solution)/shard_map/ppermute | solution.py:42
  49.0 116.7 %collective-permute-start.6 = (bf16[256,512]{0,1:T(8,128)(2,1)S(1)}, bf16[256,512]{0,1:T(8,128)(2,1)}, u32[]{:S(2)}, u32[]{:S(2)}) collective-permute-start(bf16[256,512]{0,1:T(8,128)(2,1)S(1)} %bitcast.410), channel_id=1, source_target_pairs={{0,16},{16,0},{8,24},{24,8},{1,17},{17,1},{9,25},{25,9},{2,18},{18... | collective-permute-start | bytes 786440 | tf_op jit(solution)/shard_map/ppermute | solution.py:46
  49.6 119.0 %collective-permute-start.5 = (bf16[256,512]{0,1:T(8,128)(2,1)S(1)}, bf16[256,512]{0,1:T(8,128)(2,1)}, u32[]{:S(2)}, u32[]{:S(2)}) collective-permute-start(bf16[256,512]{0,1:T(8,128)(2,1)S(1)} %bitcast.411), channel_id=1, source_target_pairs={{0,8},{8,0},{16,24},{24,16},{1,9},{9,1},{17,25},{25,17},{2,10},{10... | collective-permute-start | bytes 786440 | tf_op jit(solution)/shard_map/ppermute | solution.py:42
  75.6 115.4 %collective-permute-start.20 = (bf16[256,1536]{0,1:T(8,128)(2,1)S(1)}, bf16[256,1536]{0,1:T(8,128)(2,1)}, u32[]{:S(2)}, u32[]{:S(2)}) collective-permute-start(bf16[256,1536]{0,1:T(8,128)(2,1)S(1)} %bitcast.384), channel_id=1, source_target_pairs={{0,16},{16,0},{8,24},{24,8},{1,17},{17,1},{9,25},{25,9},{2,18},{18... | collective-permute-start | bytes 2359304 | tf_op jit(solution)/shard_map/ppermute | solution.py:46
  77.8 810.0 %all-reduce.6.cloned.1.call-start = ((), (), s32[]{:S(2)}) async-start(), calls=%async_computation.10 | async-start | bytes 163840 | tf_op jit(solution)/shard_map/psum | solution.py:317
  162.7 30.5 %collective-permute-start.19 = (bf16[256,1536]{0,1:T(8,128)(2,1)S(1)}, bf16[256,1536]{0,1:T(8,128)(2,1)S(1)}, u32[]{:S(2)}, u32[]{:S(2)}) collective-permute-start(bf16[256,1536]{0,1:T(8,128)(2,1)S(1)} %bitcast.386), channel_id=1, source_target_pairs={{0,8},{8,0},{16,24},{24,16},{1,9},{9,1},{17,25},{25,17},{2,10},{10... | collective-permute-start | bytes 2359304 | tf_op jit(solution)/shard_map/ppermute | solution.py:42
  165.7 28.9 %collective-permute-start.2 = (bf16[256,1536]{0,1:T(8,128)(2,1)S(1)}, bf16[256,1536]{0,1:T(8,128)(2,1)S(1)}, u32[]{:S(2)}, u32[]{:S(2)}) collective-permute-start(bf16[256,1536]{0,1:T(8,128)(2,1)S(1)} %bitcast.388), channel_id=1, source_target_pairs={{0,16},{16,0},{8,24},{24,8},{1,17},{17,1},{9,25},{25,9},{2,18},{18... | collective-permute-start | bytes 2359304 | tf_op jit(solution)/shard_map/ppermute | solution.py:46
  168.6 28.0 %collective-permute-start.1 = (bf16[256,1536]{0,1:T(8,128)(2,1)S(1)}, bf16[256,1536]{0,1:T(8,128)(2,1)S(1)}, u32[]{:S(2)}, u32[]{:S(2)}) collective-permute-start(bf16[256,1536]{0,1:T(8,128)(2,1)S(1)} %bitcast.389), channel_id=1, source_target_pairs={{0,8},{8,0},{16,24},{24,16},{1,9},{9,1},{17,25},{25,17},{2,10},{10... | collective-permute-start | bytes 2359304 | tf_op jit(solution)/shard_map/ppermute | solution.py:42
  190.3 24.3 %collective-permute-start = (bf16[2,320,1024]{2,1,0:T(8,128)(2,1)S(1)}, bf16[2,320,1024]{2,1,0:T(8,128)(2,1)S(1)}, u32[]{:S(2)}, u32[]{:S(2)}) collective-permute-start(bf16[2,320,1024]{2,1,0:T(8,128)(2,1)S(1)} %copy-done.64), channel_id=1, source_target_pairs={{0,4},{4,0},{1,5},{5,1},{2,6},{6,2},{3,7},{7,3},{8,12},{12,8},{9,1... | collective-permute-start | bytes 3932168 | tf_op jit(solution)/shard_map/ppermute | solution.py:50
  192.8 97.5 %collective-permute-start.22 = (bf16[128,1536]{0,1:T(8,128)(2,1)}, bf16[128,1536]{0,1:T(8,128)(2,1)S(1)}, u32[]{:S(2)}, u32[]{:S(2)}) collective-permute-start(bf16[128,1536]{0,1:T(8,128)(2,1)} %slice.877), channel_id=1, source_target_pairs={{0,8},{8,0},{16,24},{24,16},{1,9},{9,1},{17,25},{25,17},{2,10},{10... | collective-permute-start | bytes 1179656 | tf_op jit(solution)/shard_map/ppermute | solution.py:42
  290.3 31.3 %collective-permute-start.9 = (bf16[592,1024]{1,0:T(8,128)(2,1)}, bf16[592,1024]{1,0:T(8,128)(2,1)}, u32[]{:S(2)}, u32[]{:S(2)}) collective-permute-start(bf16[592,1024]{1,0:T(8,128)(2,1)} %convolution_convert_fusion.5), channel_id=1, source_target_pairs={{0,4},{4,0},{1,5},{5,1},{2,6},{6,2},{3,7},{7,3},{8,12},{12,8},{9,1... | collective-permute-start | bytes 3637256 | tf_op jit(solution)/shard_map/ppermute | solution.py:50
  302.4 60.0 %collective-permute-start.15 = (bf16[256,2048]{0,1:T(8,128)(2,1)}, bf16[256,2048]{0,1:T(8,128)(2,1)}, u32[]{:S(2)}, u32[]{:S(2)}) collective-permute-start(bf16[256,2048]{0,1:T(8,128)(2,1)} %bitcast.41), channel_id=1, source_target_pairs={{0,16},{16,0},{8,24},{24,8},{1,17},{17,1},{9,25},{25,9},{2,18},{18... | collective-permute-start | bytes 3145736 | tf_op jit(solution)/shard_map/ppermute | solution.py:46
  303.9 53.9 %collective-permute-start.14 = (bf16[256,2048]{0,1:T(8,128)(2,1)}, bf16[256,2048]{0,1:T(8,128)(2,1)}, u32[]{:S(2)}, u32[]{:S(2)}) collective-permute-start(bf16[256,2048]{0,1:T(8,128)(2,1)} %bitcast.41), channel_id=1, source_target_pairs={{0,8},{8,0},{16,24},{24,16},{1,9},{9,1},{17,25},{25,17},{2,10},{10... | collective-permute-start | bytes 3145736 | tf_op jit(solution)/shard_map/ppermute | solution.py:42
  310.3 49.3 %collective-permute-start.11 = (bf16[256,2048]{0,1:T(8,128)(2,1)}, bf16[256,2048]{0,1:T(8,128)(2,1)}, u32[]{:S(2)}, u32[]{:S(2)}) collective-permute-start(bf16[256,2048]{0,1:T(8,128)(2,1)} %bitcast.33), channel_id=1, source_target_pairs={{0,16},{16,0},{8,24},{24,8},{1,17},{17,1},{9,25},{25,9},{2,18},{18... | collective-permute-start | bytes 3145736 | tf_op jit(solution)/shard_map/ppermute | solution.py:46
  310.4 43.2 %collective-permute-start.10 = (bf16[256,2048]{0,1:T(8,128)(2,1)}, bf16[256,2048]{0,1:T(8,128)(2,1)}, u32[]{:S(2)}, u32[]{:S(2)}) collective-permute-start(bf16[256,2048]{0,1:T(8,128)(2,1)} %bitcast.33), channel_id=1, source_target_pairs={{0,8},{8,0},{16,24},{24,16},{1,9},{9,1},{17,25},{25,17},{2,10},{10... | collective-permute-start | bytes 3145736 | tf_op jit(solution)/shard_map/ppermute | solution.py:42
  321.6 103.1 %collective-permute-start.33 = (bf16[256,2048]{0,1:T(8,128)(2,1)S(1)}, bf16[256,2048]{0,1:T(8,128)(2,1)S(1)}, u32[]{:S(2)}, u32[]{:S(2)}) collective-permute-start(bf16[256,2048]{0,1:T(8,128)(2,1)S(1)} %bitcast.377), channel_id=1, source_target_pairs={{0,16},{16,0},{8,24},{24,8},{1,17},{17,1},{9,25},{25,9},{2,18},{18... | collective-permute-start | bytes 3145736 | tf_op jit(solution)/shard_map/ppermute | solution.py:46
  353.6 71.9 %collective-permute-start.32 = (bf16[256,2048]{0,1:T(8,128)(2,1)S(1)}, bf16[256,2048]{0,1:T(8,128)(2,1)S(1)}, u32[]{:S(2)}, u32[]{:S(2)}) collective-permute-start(bf16[256,2048]{0,1:T(8,128)(2,1)S(1)} %bitcast.378), channel_id=1, source_target_pairs={{0,8},{8,0},{16,24},{24,16},{1,9},{9,1},{17,25},{25,17},{2,10},{10... | collective-permute-start | bytes 3145736 | tf_op jit(solution)/shard_map/ppermute | solution.py:42
  357.8 26.9 %collective-permute-start.12 = (bf16[128,2048]{0,1:T(8,128)(2,1)S(1)}, bf16[128,2048]{0,1:T(8,128)(2,1)S(1)}, u32[]{:S(2)}, u32[]{:S(2)}) collective-permute-start(bf16[128,2048]{0,1:T(8,128)(2,1)S(1)} %slice.868), channel_id=1, source_target_pairs={{0,16},{16,0},{8,24},{24,8},{1,17},{17,1},{9,25},{25,9},{2,18},{18... | collective-permute-start | bytes 1572872 | tf_op jit(solution)/shard_map/ppermute | solution.py:46
  359.5 68.6 %collective-permute-start.29 = (bf16[256,2048]{0,1:T(8,128)(2,1)S(1)}, bf16[256,2048]{0,1:T(8,128)(2,1)S(1)}, u32[]{:S(2)}, u32[]{:S(2)}) collective-permute-start(bf16[256,2048]{0,1:T(8,128)(2,1)S(1)} %bitcast.374), channel_id=1, source_target_pairs={{0,16},{16,0},{8,24},{24,8},{1,17},{17,1},{9,25},{25,9},{2,18},{18... | collective-permute-start | bytes 3145736 | tf_op jit(solution)/shard_map/ppermute | solution.py:46
  362.4 28.5 %collective-permute-start.13 = (bf16[128,2048]{0,1:T(8,128)(2,1)S(1)}, bf16[128,2048]{0,1:T(8,128)(2,1)S(1)}, u32[]{:S(2)}, u32[]{:S(2)}) collective-permute-start(bf16[128,2048]{0,1:T(8,128)(2,1)S(1)} %slice.869), channel_id=1, source_target_pairs={{0,8},{8,0},{16,24},{24,16},{1,9},{9,1},{17,25},{25,17},{2,10},{10... | collective-permute-start | bytes 1572872 | tf_op jit(solution)/shard_map/ppermute | solution.py:42
  384.7 36.6 %collective-permute-start.17 = (bf16[128,2048]{0,1:T(8,128)(2,1)S(1)}, bf16[128,2048]{0,1:T(8,128)(2,1)S(1)}, u32[]{:S(2)}, u32[]{:S(2)}) collective-permute-start(bf16[128,2048]{0,1:T(8,128)(2,1)S(1)} %slice.872), channel_id=1, source_target_pairs={{0,8},{8,0},{16,24},{24,16},{1,9},{9,1},{17,25},{25,17},{2,10},{10... | collective-permute-start | bytes 1572872 | tf_op jit(solution)/shard_map/ppermute | solution.py:42
  390.9 27.1 %collective-permute-start.16 = (bf16[128,2048]{0,1:T(8,128)(2,1)S(1)}, bf16[128,2048]{0,1:T(8,128)(2,1)S(1)}, u32[]{:S(2)}, u32[]{:S(2)}) collective-permute-start(bf16[128,2048]{0,1:T(8,128)(2,1)S(1)} %slice.871), channel_id=1, source_target_pairs={{0,16},{16,0},{8,24},{24,8},{1,17},{17,1},{9,25},{25,9},{2,18},{18... | collective-permute-start | bytes 1572872 | tf_op jit(solution)/shard_map/ppermute | solution.py:46
  418.0 27.1 %collective-permute-start.28 = (bf16[256,2048]{0,1:T(8,128)(2,1)S(1)}, bf16[256,2048]{0,1:T(8,128)(2,1)S(1)}, u32[]{:S(2)}, u32[]{:S(2)}) collective-permute-start(bf16[256,2048]{0,1:T(8,128)(2,1)S(1)} %bitcast.375), channel_id=1, source_target_pairs={{0,8},{8,0},{16,24},{24,16},{1,9},{9,1},{17,25},{25,17},{2,10},{10... | collective-permute-start | bytes 3145736 | tf_op jit(solution)/shard_map/ppermute | solution.py:42
  425.5 51.8 %collective-permute-start.35 = (bf16[128,2048]{0,1:T(8,128)(2,1)}, bf16[128,2048]{0,1:T(8,128)(2,1)}, u32[]{:S(2)}, u32[]{:S(2)}) collective-permute-start(bf16[128,2048]{0,1:T(8,128)(2,1)} %slice.890), channel_id=1, source_target_pairs={{0,8},{8,0},{16,24},{24,16},{1,9},{9,1},{17,25},{25,17},{2,10},{10... | collective-permute-start | bytes 1572872 | tf_op jit(solution)/shard_map/ppermute | solution.py:42
  426.3 49.0 %collective-permute-start.34 = (bf16[128,2048]{0,1:T(8,128)(2,1)}, bf16[128,2048]{0,1:T(8,128)(2,1)}, u32[]{:S(2)}, u32[]{:S(2)}) collective-permute-start(bf16[128,2048]{0,1:T(8,128)(2,1)} %slice.889), channel_id=1, source_target_pairs={{0,16},{16,0},{8,24},{24,8},{1,17},{17,1},{9,25},{25,9},{2,18},{18... | collective-permute-start | bytes 1572872 | tf_op jit(solution)/shard_map/ppermute | solution.py:46
  429.0 51.6 %collective-permute-start.31 = (bf16[128,2048]{0,1:T(8,128)(2,1)}, bf16[128,2048]{0,1:T(8,128)(2,1)}, u32[]{:S(2)}, u32[]{:S(2)}) collective-permute-start(bf16[128,2048]{0,1:T(8,128)(2,1)} %slice.888), channel_id=1, source_target_pairs={{0,8},{8,0},{16,24},{24,16},{1,9},{9,1},{17,25},{25,17},{2,10},{10... | collective-permute-start | bytes 1572872 | tf_op jit(solution)/shard_map/ppermute | solution.py:42
  446.0 33.3 %collective-permute-start.30 = (bf16[128,2048]{0,1:T(8,128)(2,1)}, bf16[128,2048]{0,1:T(8,128)(2,1)}, u32[]{:S(2)}, u32[]{:S(2)}) collective-permute-start(bf16[128,2048]{0,1:T(8,128)(2,1)} %slice.887), channel_id=1, source_target_pairs={{0,16},{16,0},{8,24},{24,8},{1,17},{17,1},{9,25},{25,9},{2,18},{18... | collective-permute-start | bytes 1572872 | tf_op jit(solution)/shard_map/ppermute | solution.py:46
  501.0 63.0 %collective-permute-start.37 = (bf16[592,1024]{1,0:T(8,128)(2,1)}, bf16[592,1024]{1,0:T(8,128)(2,1)}, u32[]{:S(2)}, u32[]{:S(2)}) collective-permute-start(bf16[592,1024]{1,0:T(8,128)(2,1)} %convolution_convert_fusion.1), channel_id=1, source_target_pairs={{0,4},{4,0},{1,5},{5,1},{2,6},{6,2},{3,7},{7,3},{8,12},{12,8},{9,1... | collective-permute-start | bytes 3637256 | tf_op jit(solution)/shard_map/ppermute | solution.py:50
  502.2 55.8 %collective-permute-start.68 = (bf16[256,2048]{1,0:T(8,128)(2,1)}, bf16[256,2048]{1,0:T(8,128)(2,1)}, u32[]{:S(2)}, u32[]{:S(2)}) collective-permute-start(bf16[256,2048]{1,0:T(8,128)(2,1)} %pad_maximum_fusion.6), channel_id=1, source_target_pairs={{0,16},{16,0},{8,24},{24,8},{1,17},{17,1},{9,25},{25,9},{2,18},{18... | collective-permute-start | bytes 3145736 | tf_op jit(solution)/shard_map/ppermute | solution.py:46
  503.5 26.3 %collective-permute-start.66 = (bf16[256,2048]{1,0:T(8,128)(2,1)}, bf16[256,2048]{1,0:T(8,128)(2,1)}, u32[]{:S(2)}, u32[]{:S(2)}) collective-permute-start(bf16[256,2048]{1,0:T(8,128)(2,1)} %pad_maximum_fusion.5), channel_id=1, source_target_pairs={{0,8},{8,0},{16,24},{24,16},{1,9},{9,1},{17,25},{25,17},{2,10},{10... | collective-permute-start | bytes 3145736 | tf_op jit(solution)/shard_map/ppermute | solution.py:42
  512.8 48.5 %collective-permute-start.78 = (bf16[256,2048]{1,0:T(8,128)(2,1)}, bf16[256,2048]{1,0:T(8,128)(2,1)}, u32[]{:S(2)}, u32[]{:S(2)}) collective-permute-start(bf16[256,2048]{1,0:T(8,128)(2,1)} %pad_maximum_fusion.10), channel_id=1, source_target_pairs={{0,16},{16,0},{8,24},{24,8},{1,17},{17,1},{9,25},{25,9},{2,18},{18... | collective-permute-start | bytes 3145736 | tf_op jit(solution)/shard_map/ppermute | solution.py:46
  515.6 36.3 %collective-permute-start.76 = (bf16[256,2048]{1,0:T(8,128)(2,1)}, bf16[256,2048]{1,0:T(8,128)(2,1)}, u32[]{:S(2)}, u32[]{:S(2)}) collective-permute-start(bf16[256,2048]{1,0:T(8,128)(2,1)} %pad_maximum_fusion.9), channel_id=1, source_target_pairs={{0,8},{8,0},{16,24},{24,16},{1,9},{9,1},{17,25},{25,17},{2,10},{10... | collective-permute-start | bytes 3145736 | tf_op jit(solution)/shard_map/ppermute | solution.py:42
  529.8 37.1 %collective-permute-start.36 = (bf16[592,1024]{1,0:T(8,128)(2,1)}, bf16[592,1024]{1,0:T(8,128)(2,1)S(1)}, u32[]{:S(2)}, u32[]{:S(2)}) collective-permute-start(bf16[592,1024]{1,0:T(8,128)(2,1)} %convolution_convert_fusion.2), channel_id=1, source_target_pairs={{0,4},{4,0},{1,5},{5,1},{2,6},{6,2},{3,7},{7,3},{8,12},{12,8},{9,1... | collective-permute-start | bytes 3637256 | tf_op jit(solution)/shard_map/ppermute | solution.py:50
  551.9 90.3 %collective-permute-start.67 = (bf16[128,2048]{1,0:T(8,128)(2,1)}, bf16[128,2048]{1,0:T(8,128)(2,1)}, u32[]{:S(2)}, u32[]{:S(2)}) collective-permute-start(bf16[128,2048]{1,0:T(8,128)(2,1)} %fusion.48), channel_id=1, source_target_pairs={{0,16},{16,0},{8,24},{24,8},{1,17},{17,1},{9,25},{25,9},{2,18},{18... | collective-permute-start | bytes 1572872 | tf_op jit(solution)/shard_map/ppermute | solution.py:46
  558.1 185.1 %collective-permute-start.77 = (bf16[128,2048]{1,0:T(8,128)(2,1)}, bf16[128,2048]{1,0:T(8,128)(2,1)}, u32[]{:S(2)}, u32[]{:S(2)}) collective-permute-start(bf16[128,2048]{1,0:T(8,128)(2,1)} %fusion.36), channel_id=1, source_target_pairs={{0,16},{16,0},{8,24},{24,8},{1,17},{17,1},{9,25},{25,9},{2,18},{18... | collective-permute-start | bytes 1572872 | tf_op jit(solution)/shard_map/ppermute | solution.py:46
  636.2 26.1 %collective-permute-start.38 = (bf16[592,1024]{1,0:T(8,128)(2,1)}, bf16[592,1024]{1,0:T(8,128)(2,1)}, u32[]{:S(2)}, u32[]{:S(2)}) collective-permute-start(bf16[592,1024]{1,0:T(8,128)(2,1)} %convolution_convert_fusion.7), channel_id=1, source_target_pairs={{0,4},{4,0},{1,5},{5,1},{2,6},{6,2},{3,7},{7,3},{8,12},{12,8},{9,1... | collective-permute-start | bytes 3637256 | tf_op jit(solution)/shard_map/ppermute | solution.py:50
  637.2 120.8 %collective-permute-start.48 = (bf16[256,1536]{1,0:T(8,128)(2,1)}, bf16[256,1536]{1,0:T(8,128)(2,1)}, u32[]{:S(2)}, u32[]{:S(2)}) collective-permute-start(bf16[256,1536]{1,0:T(8,128)(2,1)} %pad_maximum_fusion.18), channel_id=1, source_target_pairs={{0,16},{16,0},{8,24},{24,8},{1,17},{17,1},{9,25},{25,9},{2,18},{18... | collective-permute-start | bytes 2359304 | tf_op jit(solution)/shard_map/ppermute | solution.py:46
  639.3 114.5 %collective-permute-start.46 = (bf16[256,1536]{1,0:T(8,128)(2,1)}, bf16[256,1536]{1,0:T(8,128)(2,1)}, u32[]{:S(2)}, u32[]{:S(2)}) collective-permute-start(bf16[256,1536]{1,0:T(8,128)(2,1)} %pad_maximum_fusion.17), channel_id=1, source_target_pairs={{0,8},{8,0},{16,24},{24,16},{1,9},{9,1},{17,25},{25,17},{2,10},{10... | collective-permute-start | bytes 2359304 | tf_op jit(solution)/shard_map/ppermute | solution.py:42
  660.2 74.7 %collective-permute-start.69 = (bf16[128,2048]{1,0:T(8,128)(2,1)}, bf16[128,2048]{1,0:T(8,128)(2,1)}, u32[]{:S(2)}, u32[]{:S(2)}) collective-permute-start(bf16[128,2048]{1,0:T(8,128)(2,1)} %get-tuple-element.105), channel_id=1, source_target_pairs={{0,8},{8,0},{16,24},{24,16},{1,9},{9,1},{17,25},{25,17},{2,10},{10... | collective-permute-start | bytes 1572872 | tf_op jit(solution)/shard_map/ppermute | solution.py:42
  734.1 239.5 %reduce-scatter.15.cloned.1.call-start = ((), (), s32[]{:S(2)}) async-start(), calls=%async_computation.13 | async-start | bytes 327680 | tf_op jit(solution)/shard_map/reduce_scatter | solution.py:101
  734.9 238.8 %reduce-scatter.19.cloned.1.call-start = ((), (), s32[]{:S(2)}) async-start(), calls=%async_computation.15 | async-start | bytes 1310720 | tf_op jit(solution)/shard_map/reduce_scatter | solution.py:101
  743.1 231.1 %reduce-scatter.23.cloned.1.call-start = ((), (), s32[]{:S(2)}) async-start(), calls=%async_computation.17 | async-start | bytes 1310720 | tf_op jit(solution)/shard_map/reduce_scatter | solution.py:101
  769.2 206.8 %reduce-scatter.11.cloned.1.call-start = ((), (), s32[]{:S(2)}) async-start(), calls=%async_computation.9 | async-start | bytes 983040 | tf_op jit(solution)/shard_map/reduce_scatter | solution.py:101
  774.9 25.4 %collective-permute-start.49 = (bf16[128,1536]{1,0:T(8,128)(2,1)}, bf16[128,1536]{1,0:T(8,128)(2,1)S(1)}, u32[]{:S(2)}, u32[]{:S(2)}) collective-permute-start(bf16[128,1536]{1,0:T(8,128)(2,1)} %get-tuple-element.109), channel_id=1, source_target_pairs={{0,8},{8,0},{16,24},{24,16},{1,9},{9,1},{17,25},{25,17},{2,10},{10... | collective-permute-start | bytes 1179656 | tf_op jit(solution)/shard_map/ppermute | solution.py:42
  786.8 52.7 %collective-permute-start.63 = (bf16[256,2048]{1,0:T(8,128)(2,1)}, bf16[256,2048]{1,0:T(8,128)(2,1)}, u32[]{:S(2)}, u32[]{:S(2)}) collective-permute-start(bf16[256,2048]{1,0:T(8,128)(2,1)} %pad_maximum_fusion.4), channel_id=1, source_target_pairs={{0,16},{16,0},{8,24},{24,8},{1,17},{17,1},{9,25},{25,9},{2,18},{18... | collective-permute-start | bytes 3145736 | tf_op jit(solution)/shard_map/ppermute | solution.py:46
  789.3 26.4 %collective-permute-start.61 = (bf16[256,2048]{1,0:T(8,128)(2,1)}, bf16[256,2048]{1,0:T(8,128)(2,1)}, u32[]{:S(2)}, u32[]{:S(2)}) collective-permute-start(bf16[256,2048]{1,0:T(8,128)(2,1)} %pad_maximum_fusion.3), channel_id=1, source_target_pairs={{0,8},{8,0},{16,24},{24,16},{1,9},{9,1},{17,25},{25,17},{2,10},{10... | collective-permute-start | bytes 3145736 | tf_op jit(solution)/shard_map/ppermute | solution.py:42
  797.0 45.6 %collective-permute-start.73 = (bf16[256,2048]{1,0:T(8,128)(2,1)}, bf16[256,2048]{1,0:T(8,128)(2,1)}, u32[]{:S(2)}, u32[]{:S(2)}) collective-permute-start(bf16[256,2048]{1,0:T(8,128)(2,1)} %pad_maximum_fusion.8), channel_id=1, source_target_pairs={{0,16},{16,0},{8,24},{24,8},{1,17},{17,1},{9,25},{25,9},{2,18},{18... | collective-permute-start | bytes 3145736 | tf_op jit(solution)/shard_map/ppermute | solution.py:46
  799.2 36.9 %collective-permute-start.71 = (bf16[256,2048]{1,0:T(8,128)(2,1)}, bf16[256,2048]{1,0:T(8,128)(2,1)}, u32[]{:S(2)}, u32[]{:S(2)}) collective-permute-start(bf16[256,2048]{1,0:T(8,128)(2,1)} %pad_maximum_fusion.7), channel_id=1, source_target_pairs={{0,8},{8,0},{16,24},{24,16},{1,9},{9,1},{17,25},{25,17},{2,10},{10... | collective-permute-start | bytes 3145736 | tf_op jit(solution)/shard_map/ppermute | solution.py:42
  805.5 172.8 %reduce-scatter.13.cloned.1.call-start = ((), (), s32[]{:S(2)}) async-start(), calls=%async_computation.12 | async-start | bytes 327680 | tf_op jit(solution)/shard_map/reduce_scatter | solution.py:101
  820.0 72.7 %collective-permute-start.62 = (bf16[128,2048]{1,0:T(8,128)(2,1)}, bf16[128,2048]{1,0:T(8,128)(2,1)}, u32[]{:S(2)}, u32[]{:S(2)}) collective-permute-start(bf16[128,2048]{1,0:T(8,128)(2,1)} %fusion.54), channel_id=1, source_target_pairs={{0,16},{16,0},{8,24},{24,8},{1,17},{17,1},{9,25},{25,9},{2,18},{18... | collective-permute-start | bytes 1572872 | tf_op jit(solution)/shard_map/ppermute | solution.py:46
  882.7 98.8 %all-reduce.8.cloned.1.call-start = ((), (), s32[]{:S(2)}) async-start(), calls=%async_computation.11 | async-start | bytes 163840 | tf_op jit(solution)/shard_map/psum | solution.py:316
  887.8 94.6 %reduce-scatter.21.cloned.1.call-start = ((), (), s32[]{:S(2)}) async-start(), calls=%async_computation.16 | async-start | bytes 1310720 | tf_op jit(solution)/shard_map/reduce_scatter | solution.py:101
  890.0 119.1 %reduce-scatter.17.cloned.1.call-start = ((), (), s32[]{:S(2)}) async-start(), calls=%async_computation.14 | async-start | bytes 1310720 | tf_op jit(solution)/shard_map/reduce_scatter | solution.py:101
  898.8 33.9 %collective-permute-start.43 = (bf16[256,1536]{1,0:T(8,128)(2,1)}, bf16[256,1536]{1,0:T(8,128)(2,1)}, u32[]{:S(2)}, u32[]{:S(2)}) collective-permute-start(bf16[256,1536]{1,0:T(8,128)(2,1)} %pad_maximum_fusion.16), channel_id=1, source_target_pairs={{0,16},{16,0},{8,24},{24,8},{1,17},{17,1},{9,25},{25,9},{2,18},{18... | collective-permute-start | bytes 2359304 | tf_op jit(solution)/shard_map/ppermute | solution.py:46
  924.7 109.1 %reduce-scatter.9.cloned.1.call-start = ((), (), s32[]{:S(2)}) async-start(), calls=%async_computation.8 | async-start | bytes 983040 | tf_op jit(solution)/shard_map/reduce_scatter | solution.py:101
  949.7 140.2 %all-gather.29.cloned.1.call-start = ((), (), s32[]{:S(2)}) async-start(), calls=%async_computation.23 | async-start | bytes 3276800 | tf_op jit(solution)/shard_map/all_gather | solution.py:289
  973.0 171.9 %all-gather.27.cloned.1.call-start = ((), (), s32[]{:S(2)}) async-start(), calls=%async_computation.22 | async-start | bytes 3276800 | tf_op jit(solution)/shard_map/all_gather | solution.py:289
  982.4 51.4 %collective-permute-start.75 = (bf16[256,1,512]{2,0,1:T(8,128)(2,1)}, bf16[256,1,512]{2,0,1:T(8,128)(2,1)S(1)}, u32[]{:S(2)}, u32[]{:S(2)}) collective-permute-start(bf16[256,1,512]{2,0,1:T(8,128)(2,1)} %bitcast.440), channel_id=1, source_target_pairs={{0,4},{4,0},{1,5},{5,1},{2,6},{6,2},{3,7},{7,3},{8,12},{12,8},{9,1... | collective-permute-start | bytes 786440 | tf_op jit(solution)/shard_map/ppermute | solution.py:50
  1009.1 26.0 %collective-permute-start.65 = (bf16[256,1,512]{2,0,1:T(8,128)(2,1)}, bf16[256,1,512]{2,0,1:T(8,128)(2,1)}, u32[]{:S(2)}, u32[]{:S(2)}) collective-permute-start(bf16[256,1,512]{2,0,1:T(8,128)(2,1)} %bitcast.441), channel_id=1, source_target_pairs={{0,4},{4,0},{1,5},{5,1},{2,6},{6,2},{3,7},{7,3},{8,12},{12,8},{9,1... | collective-permute-start | bytes 786440 | tf_op jit(solution)/shard_map/ppermute | solution.py:50
  (164 other events, 1974.7 us)
Sparse Core Ops, SparseCore 0:
  10.2 36.8 all-gather.20
  49.2 35.7 all-gather.18
  87.1 36.1 all-gather.22
  124.7 30.9 all-gather.24
  734.2 47.0 all-reduce.5
  783.5 22.8 reduce-scatter.14
  808.7 25.3 reduce-scatter.18
  836.5 25.8 reduce-scatter.22
  864.6 21.9 reduce-scatter.10
  888.7 18.9 reduce-scatter.12
  910.9 39.3 all-reduce.7
  952.4 27.8 reduce-scatter.20
  983.3 25.7 reduce-scatter.16
  1011.8 21.9 reduce-scatter.8
  1035.8 54.0 all-gather.28
  1091.3 53.5 all-gather.26
